TPU v7x, 32 devices: a whole 2x2x4 slice. The times are simulated.
32 devices in a mesh: tower: 2 (over core), batch: 16 (over z, y, x).
Axes of the slice: x: 2, y: 2, z: 4, core: 2. Of those that a mesh axis runs over, the one named last changes fastest.
Arguments:
- tokens: bfloat16 [2, 16, 512, 768], P('tower', 'batch'), may hold values from -6 to 6
- segments: int32 [2, 16, 512], P('tower', 'batch'), may hold values from 0 to 8, as said below
- w_query: bfloat16 [768, 768], replicated, may hold values from -0.02734375 to 0.02734375
- w_key: bfloat16 [768, 768], replicated, may hold values from -0.21875 to 0.21875
- w_value: bfloat16 [768, 768], replicated, may hold values from -0.21875 to 0.21875
- w_output: bfloat16 [768, 768], replicated, may hold values from -0.875 to 0.875
- w_gate: bfloat16 [768, 3072], replicated, may hold values from -0.21875 to 0.21875
- w_up: bfloat16 [768, 3072], replicated, may hold values from -0.21875 to 0.21875
- w_down: bfloat16 [3072, 768], replicated, may hold values from -0.15625 to 0.15625
- gain_attn: float32 [768], replicated, may hold values from 0.25 to 1.75
- gain_ffn: float32 [768], replicated, may hold values from 0.25 to 1.75
- gain_final: float32 [768], replicated, may hold values from 0.25 to 1.75
- bias_table: float32 [32, 12], replicated, may hold values from -4 to 4
- out_grad: bfloat16 [2, 16, 512, 768], P('tower', 'batch'), may hold values from -6 to 6
- score_grad: float32 [128, 128], P('batch'), may hold values from -6 to 6
Outputs:
- output: bfloat16 [2, 16, 512, 768], P('tower', 'batch')
- scores: float32 [128, 128], P('batch')
- grad_tokens: bfloat16 [2, 16, 512, 768], P('tower', 'batch')
- grad_w_query: float32 [768, 768], P(None, 'batch')
- grad_w_key: float32 [768, 768], P(None, 'batch')
- grad_w_value: float32 [768, 768], P(None, 'batch')
- grad_w_output: float32 [768, 768], P(None, 'batch')
- grad_w_gate: float32 [768, 3072], P(None, 'batch')
- grad_w_up: float32 [768, 3072], P(None, 'batch')
- grad_w_down: float32 [3072, 768], P(None, 'batch')
- grad_gain_attn: float32 [768], P('batch')
- grad_gain_ffn: float32 [768], P('batch')
- grad_gain_final: float32 [768], P('batch')
- grad_bias_table: float32 [32, 12], replicated
Inputs may be any that keep to these rules, and one draw needn't show every extreme that they name: `segments`: each row of 512 tokens holds the items 1 to 8 in this order, each a run of one or more tokens, followed by one or more padding tokens of id 0.
All inputs are finite; a program needn't handle non-finite values.
Results may differ from a plain program's by a relative error of at most 0.015.
Values may be sent and summed in bfloat16 or wider, within the bound.
No kernel may reach another device: no remote copies, remote signals or barrier semaphores. Data moves between devices by JAX's collectives and lax.ppermute only.
A program may use at most 256 MiB of HBM per device.

v0:
```python
import jax
import jax.numpy as jnp
import numpy as np
from jax import lax
from jax.sharding import PartitionSpec as P

ITEMS = 8


eps_norm = 1e-06
temper = 0.05
max_distance = 128
highest = lax.Precision.HIGHEST
masked_value = -1000000000.0
contract_rows = (((0,), (0,)), ((), ()))
contract_cols = (((1,), (1,)), ((), ()))


def bucket_table(length, bucket_count):
    relative = np.arange(length)[None, :] - np.arange(length)[:, None]
    halfway = bucket_count // 2
    upper_part = np.where(relative > 0, halfway, 0)
    distance = np.abs(relative)
    exact_span = halfway // 2
    scaled = (
        np.log(np.maximum(distance, 1) / exact_span)
        / np.log(max_distance / exact_span)
        * (halfway - exact_span)
    )
    far_bucket = np.minimum(
        exact_span + np.floor(np.maximum(scaled, 0.0)).astype(np.int32), halfway - 1
    )
    return (upper_part + np.where(distance < exact_span, distance, far_bucket)).astype(np.int32)


def rms_scale(values):
    return lax.rsqrt(jnp.mean(values * values, axis=-1, keepdims=True) + eps_norm)


def norm_back(values, scale, gain, grad_normed):
    scaled_grad = grad_normed * gain
    grad_values = scale * scaled_grad - values * scale**3 * jnp.mean(
        scaled_grad * values, axis=-1, keepdims=True
    )
    grad_gain = jnp.sum(grad_normed * values * scale, axis=0)
    return (grad_values, grad_gain)


def gelu_tanh(values):
    return jax.nn.gelu(values, approximate=True)


def project(left, right):
    return jnp.dot(left, right, preferred_element_type=jnp.float32)


def body(
    tokens,
    segments,
    w_query,
    w_key,
    w_value,
    w_output,
    w_gate,
    w_up,
    w_down,
    gain_attn,
    gain_ffn,
    gain_final,
    bias_table,
    out_grad,
    score_grad,
):
    rows_here = tokens.shape[1]
    length = tokens.shape[2]
    model_width = tokens.shape[3]
    head_count = bias_table.shape[1]
    head_size = model_width // head_count
    bucket_count = bias_table.shape[0]
    token_count = rows_here * length
    row_shape = (rows_here, length, head_count, head_size)
    inputs = tokens.reshape(token_count, model_width).astype(jnp.float32)
    segment = segments.reshape(rows_here, length)
    bucket_ids = jnp.asarray(bucket_table(length, bucket_count))
    bucket_hot = bucket_ids[:, :, None] == jnp.arange(bucket_count, dtype=jnp.int32)[None, None, :]
    bias_full = jnp.einsum(
        "ijb,bh->hij", bucket_hot.astype(jnp.float32), bias_table, precision=highest
    )
    hot_low = bucket_hot.astype(jnp.bfloat16)

    def scores_of(query_row, key_row, segment_row):
        logits = (
            jnp.einsum("ihd,jhd->hij", query_row, key_row, preferred_element_type=jnp.float32)
            + bias_full
        )
        same_item = segment_row[:, None] == segment_row[None, :]
        return jnp.where(same_item[None], logits, masked_value)

    def attend(operands):
        query_row, key_row, value_row, segment_row = operands
        logits = scores_of(query_row, key_row, segment_row)
        row_peak = jnp.max(logits, axis=-1, keepdims=True)
        log_total = row_peak + jnp.log(jnp.sum(jnp.exp(logits - row_peak), axis=-1, keepdims=True))
        probs_low = jnp.exp(logits - log_total).astype(jnp.bfloat16)
        mixed_row = jnp.einsum(
            "hij,jhd->ihd", probs_low, value_row, preferred_element_type=jnp.float32
        )
        return (mixed_row.astype(jnp.bfloat16), log_total)

    def attend_back(operands):
        query_row, key_row, value_row, segment_row, log_row, grad_row = operands
        logits = scores_of(query_row, key_row, segment_row)
        attn_probs = jnp.exp(logits - log_row)
        probs_low = attn_probs.astype(jnp.bfloat16)
        grad_probs = jnp.einsum(
            "ihd,jhd->hij", grad_row, value_row, preferred_element_type=jnp.float32
        )
        inner_sum = jnp.sum(attn_probs * grad_probs, axis=-1, keepdims=True)
        grad_logits = (attn_probs * (grad_probs - inner_sum)).astype(jnp.bfloat16)
        grad_query_row = jnp.einsum(
            "hij,jhd->ihd", grad_logits, key_row, preferred_element_type=jnp.float32
        )
        grad_key_row = jnp.einsum(
            "hij,ihd->jhd", grad_logits, query_row, preferred_element_type=jnp.float32
        )
        grad_value_row = jnp.einsum(
            "hij,ihd->jhd", probs_low, grad_row, preferred_element_type=jnp.float32
        )
        grad_bias_row = jnp.einsum(
            "hij,ijb->bh", grad_logits, hot_low, preferred_element_type=jnp.float32
        )
        return (
            grad_query_row.astype(jnp.bfloat16),
            grad_key_row.astype(jnp.bfloat16),
            grad_value_row.astype(jnp.bfloat16),
            grad_bias_row,
        )

    scale_one = rms_scale(inputs)
    normed = (inputs * scale_one * gain_attn).astype(jnp.bfloat16)
    query_heads = project(normed, w_query).astype(jnp.bfloat16).reshape(row_shape)
    key_heads = project(normed, w_key).astype(jnp.bfloat16).reshape(row_shape)
    value_heads = project(normed, w_value).astype(jnp.bfloat16).reshape(row_shape)
    mixed_heads, log_totals = lax.map(attend, (query_heads, key_heads, value_heads, segment))
    mixed = mixed_heads.reshape(token_count, model_width)
    middle = inputs + project(mixed, w_output)
    scale_two = rms_scale(middle)
    normed_ffn = (middle * scale_two * gain_ffn).astype(jnp.bfloat16)
    gate_proj = project(normed_ffn, w_gate)
    up_proj = project(normed_ffn, w_up)
    activated, gelu_pull = jax.vjp(gelu_tanh, gate_proj)
    hidden = (activated * up_proj).astype(jnp.bfloat16)
    output_full = middle + project(hidden, w_down)
    output = output_full.astype(jnp.bfloat16).reshape(tokens.shape)
    scale_three = rms_scale(output_full)
    final_norm = output_full * scale_three * gain_final
    member = (
        segment[:, None, :] == jnp.arange(1, ITEMS + 1, dtype=jnp.int32)[None, :, None]
    ).astype(jnp.float32)
    counts = jnp.sum(member, axis=-1, keepdims=True)
    pooled = (
        jnp.einsum(
            "rkl,rld->rkd",
            member,
            final_norm.reshape(rows_here, length, model_width),
            precision=highest,
        )
        / counts
    )
    inv_length = lax.rsqrt(jnp.sum(pooled * pooled, axis=-1, keepdims=True) + eps_norm)
    own_items = rows_here * ITEMS
    unit_vec = (pooled * inv_length).reshape(own_items, model_width).astype(jnp.bfloat16)
    gathered = lax.all_gather(unit_vec, ("tower", "batch"), axis=0, tiled=True)
    total_items = gathered.shape[0] // 2
    query_units = lax.dynamic_slice_in_dim(
        gathered, lax.axis_index("batch") * own_items, own_items, 0
    )
    doc_units = gathered[total_items:]
    scores = (
        lax.dot_general(query_units, doc_units, contract_cols, preferred_element_type=jnp.float32)
        / temper
    )
    toward_query = jnp.dot(score_grad, doc_units.astype(jnp.float32), precision=highest) / temper
    doc_terms = (
        lax.dot_general(
            score_grad, query_units.astype(jnp.float32), contract_rows, precision=highest
        )
        / temper
    )
    toward_doc = lax.psum_scatter(doc_terms, "batch", scatter_dimension=0, tiled=True)
    grad_unit = jnp.where(lax.axis_index("tower") == 0, toward_query, toward_doc).reshape(
        rows_here, ITEMS, model_width
    )
    grad_pooled = inv_length * grad_unit - pooled * inv_length**3 * jnp.sum(
        grad_unit * pooled, axis=-1, keepdims=True
    )
    grad_final = jnp.einsum(
        "rkl,rkd->rld", member, grad_pooled / counts, precision=highest
    ).reshape(token_count, model_width)
    grad_back, grad_gain_final = norm_back(output_full, scale_three, gain_final, grad_final)
    grad_output = out_grad.reshape(token_count, model_width).astype(jnp.float32) + grad_back
    ffn_grad = grad_output.astype(jnp.bfloat16)
    grad_w_down = lax.dot_general(
        hidden, ffn_grad, contract_rows, preferred_element_type=jnp.float32
    )
    grad_hidden = lax.dot_general(
        ffn_grad, w_down, contract_cols, preferred_element_type=jnp.float32
    )
    grad_gate = gelu_pull(grad_hidden * up_proj)[0].astype(jnp.bfloat16)
    grad_up = (grad_hidden * activated).astype(jnp.bfloat16)
    grad_w_gate = lax.dot_general(
        normed_ffn, grad_gate, contract_rows, preferred_element_type=jnp.float32
    )
    grad_w_up = lax.dot_general(
        normed_ffn, grad_up, contract_rows, preferred_element_type=jnp.float32
    )
    grad_normed_ffn = lax.dot_general(
        grad_gate, w_gate, contract_cols, preferred_element_type=jnp.float32
    ) + lax.dot_general(grad_up, w_up, contract_cols, preferred_element_type=jnp.float32)
    grad_mid_norm, grad_gain_ffn = norm_back(middle, scale_two, gain_ffn, grad_normed_ffn)
    grad_middle = grad_output + grad_mid_norm
    attn_grad = grad_middle.astype(jnp.bfloat16)
    grad_w_output = lax.dot_general(
        mixed, attn_grad, contract_rows, preferred_element_type=jnp.float32
    )
    grad_mixed = lax.dot_general(
        attn_grad, w_output, contract_cols, preferred_element_type=jnp.float32
    )
    grad_mixed = grad_mixed.astype(jnp.bfloat16).reshape(row_shape)
    grad_query, grad_key, grad_value, grad_bias_rows = lax.map(
        attend_back, (query_heads, key_heads, value_heads, segment, log_totals, grad_mixed)
    )
    grad_query = grad_query.reshape(token_count, model_width)
    grad_key = grad_key.reshape(token_count, model_width)
    grad_value = grad_value.reshape(token_count, model_width)
    grad_bias_local = jnp.sum(grad_bias_rows, axis=0)
    grad_w_query = lax.dot_general(
        normed, grad_query, contract_rows, preferred_element_type=jnp.float32
    )
    grad_w_key = lax.dot_general(
        normed, grad_key, contract_rows, preferred_element_type=jnp.float32
    )
    grad_w_value = lax.dot_general(
        normed, grad_value, contract_rows, preferred_element_type=jnp.float32
    )
    grad_normed = (
        lax.dot_general(grad_query, w_query, contract_cols, preferred_element_type=jnp.float32)
        + lax.dot_general(grad_key, w_key, contract_cols, preferred_element_type=jnp.float32)
        + lax.dot_general(grad_value, w_value, contract_cols, preferred_element_type=jnp.float32)
    )
    grad_in, grad_gain_attn = norm_back(inputs, scale_one, gain_attn, grad_normed)
    grad_tokens = (grad_middle + grad_in).astype(jnp.bfloat16).reshape(tokens.shape)
    columns = (
        lax.psum_scatter(grad_w_query, "batch", scatter_dimension=1, tiled=True),
        lax.psum_scatter(grad_w_key, "batch", scatter_dimension=1, tiled=True),
        lax.psum_scatter(grad_w_value, "batch", scatter_dimension=1, tiled=True),
        lax.psum_scatter(grad_w_output, "batch", scatter_dimension=1, tiled=True),
        lax.psum_scatter(grad_w_gate, "batch", scatter_dimension=1, tiled=True),
        lax.psum_scatter(grad_w_up, "batch", scatter_dimension=1, tiled=True),
        lax.psum_scatter(grad_w_down, "batch", scatter_dimension=1, tiled=True),
        lax.psum_scatter(grad_gain_attn, "batch", scatter_dimension=0, tiled=True),
        lax.psum_scatter(grad_gain_ffn, "batch", scatter_dimension=0, tiled=True),
        lax.psum_scatter(grad_gain_final, "batch", scatter_dimension=0, tiled=True),
    )
    summed = (
        lax.psum(columns[0].astype(jnp.bfloat16), "tower").astype(jnp.float32),
        lax.psum(columns[1].astype(jnp.bfloat16), "tower").astype(jnp.float32),
        lax.psum(columns[2].astype(jnp.bfloat16), "tower").astype(jnp.float32),
        lax.psum(columns[3].astype(jnp.bfloat16), "tower").astype(jnp.float32),
        lax.psum(columns[4].astype(jnp.bfloat16), "tower").astype(jnp.float32),
        lax.psum(columns[5].astype(jnp.bfloat16), "tower").astype(jnp.float32),
        lax.psum(columns[6].astype(jnp.bfloat16), "tower").astype(jnp.float32),
        lax.psum(columns[7].astype(jnp.bfloat16), "tower").astype(jnp.float32),
        lax.psum(columns[8].astype(jnp.bfloat16), "tower").astype(jnp.float32),
        lax.psum(columns[9].astype(jnp.bfloat16), "tower").astype(jnp.float32),
    )
    grad_bias_table = lax.psum(grad_bias_local, ("tower", "batch"))
    return (
        output,
        scores,
        grad_tokens,
        summed[0],
        summed[1],
        summed[2],
        summed[3],
        summed[4],
        summed[5],
        summed[6],
        summed[7],
        summed[8],
        summed[9],
        grad_bias_table,
    )


def solution(mesh):
    in_specs = (
        P("tower", "batch", None, None),
        P("tower", "batch", None),
        P(),
        P(),
        P(),
        P(),
        P(),
        P(),
        P(),
        P(),
        P(),
        P(),
        P(),
        P("tower", "batch", None, None),
        P("batch", None),
    )
    out_specs = (
        P("tower", "batch", None, None),
        P("batch", None),
        P("tower", "batch", None, None),
        P(None, "batch"),
        P(None, "batch"),
        P(None, "batch"),
        P(None, "batch"),
        P(None, "batch"),
        P(None, "batch"),
        P(None, "batch"),
        P("batch"),
        P("batch"),
        P("batch"),
        P(),
    )
    return jax.shard_map(body, mesh=mesh, in_specs=in_specs, out_specs=out_specs, check_vma=False)
```

profile of v0, /device:TPU:0, one launch (start us, length us, event | category | flops | bytes accessed | tf_op | source)
XLA Modules:
  0.0 1431.3 jit_solution(9173081365181142992)
XLA Ops:
  21.4 15.1 %fusion.1 = f32[512,512,12]{1,2,0:T(8,128)} fusion(s32[512,512]{1,0:T(8,128)} %constant.96.clone, f32[32,12]{0,1:T(8,128)S(1)} %copy-done.41), kind=kOutput, calls=%fused_computation.2 | convolution fusion | flops 1216348160 | bytes 13633024 | tf_op jit(solution)/shard_map/ijb,bh->hij/dot_general | solution.py:86
  36.6 17.7 %copy.70 = f32[512,512,12]{0,1,2:T(8,128)} copy(f32[512,512,12]{1,2,0:T(8,128)} %fusion.1) | data formatting | bytes 25165824 | tf_op jit(solution)/shard_map/ijb,bh->hij/dot_general | solution.py:86
  54.3 6.7 fusion.94
  62.9 3.4 copy-done.1
  73.0 5.5 multiply_convert_fusion.2
  78.6 2.7 multiply_reduce_fusion.5
  83.9 77.0 %all_gather.3 = bf16[256,768]{1,0:T(8,128)(2,1)} all-gather(bf16[8,768]{1,0:T(8,128)(2,1)S(1)} %multiply_convert_fusion.4), channel_id=1, replica_groups=mesh['tower'=2,'batch'=16] {'tower','batch'}, dimensions={0}, use_global_device_ids=true | all-gather | bytes 405504 | tf_op jit(solution)/shard_map/all_gather | solution.py:173
  163.0 117.4 %reduce-scatter.9.cloned.1.call-done = f32[8,768]{1,0:T(8,128)} async-done(((f32[128,768]{1,0:T(8,128)}), f32[8,768]{1,0:T(8,128)}) %reduce-scatter.9.cloned.1.call-update) | async-done | bytes 24592 | tf_op jit(solution)/shard_map/reduce_scatter | solution.py:190
  284.3 3.5 convert_add_fusion
  287.8 10.4 multiply_convert_fusion.1
  298.3 2.7 fusion.96
  301.1 2.9 multiply_reduce_fusion.2
  308.2 3.4 convolution_convert_fusion
  314.0 6.9 fusion.41
  324.2 8.1 multiply_reduce_fusion
  332.2 7.0 multiply_convert_fusion
  345.2 5.1 convolution_convert_fusion.4
  353.5 7.1 fusion.58
  361.7 8.2 fusion.100
  370.0 8.2 fusion.99
  380.9 14.4 %copy.77 = bf16[12,512,512]{2,0,1:T(8,128)(2,1)} copy(bf16[12,512,512]{1,2,0:T(8,128)(2,1)} %copy-done.2) | data formatting | bytes 12582912 | tf_op jit(solution)/shard_map/while/body/eval_jaxpr/convert_element_type | solution.py:119
  401.0 75.0 %all-reduce.3 = (bf16[768]{0:T(1024)(128)(2,1)S(1)}, bf16[768]{0:T(1024)(128)(2,1)S(1)}, bf16[768]{0:T(1024)(128)(2,1)S(1)}) all-reduce(f32[768]{0:T(1024)S(1)} %get-tuple-element.68, f32[768]{0:T(1024)S(1)} %get-tuple-element.66, f32[768]{0:T(1024)S(1)} %copy-done.38), channel_id=10, replica_groups=mesh['tower'=2,'batch'=16] {'batch'}, use_global_device_ids=true, to_apply=%region_28.29.clone | all-reduce | flops 2304 | bytes 13824
  476.2 2.7 all-reduce.4
  482.0 86.1 %reduce-scatter.15.cloned.1.call-done = f32[768,48]{0,1:T(8,128)} async-done(((f32[768,768]{0,1:T(8,128)}), f32[768,48]{0,1:T(8,128)}) %reduce-scatter.15.cloned.1.call-update) | async-done | bytes 147472 | tf_op jit(solution)/shard_map/reduce_scatter | solution.py:256
  569.7 131.7 %reduce-scatter.11.cloned.1.call-done = f32[768,48]{0,1:T(8,128)} async-done(((f32[768,768]{0,1:T(8,128)}), f32[768,48]{0,1:T(8,128)}) %reduce-scatter.11.cloned.1.call-update) | async-done | bytes 147472 | tf_op jit(solution)/shard_map/reduce_scatter | solution.py:254
  702.9 130.9 %reduce-scatter.13.cloned.1.call-done = f32[768,48]{0,1:T(8,128)} async-done(((f32[768,768]{0,1:T(8,128)}), f32[768,48]{0,1:T(8,128)}) %reduce-scatter.13.cloned.1.call-update) | async-done | bytes 147472 | tf_op jit(solution)/shard_map/reduce_scatter | solution.py:255
  835.3 174.9 %reduce-scatter.23.cloned.1.call-done = f32[3072,48]{0,1:T(8,128)} async-done(((f32[3072,768]{0,1:T(8,128)}), f32[3072,48]{0,1:T(8,128)}) %reduce-scatter.23.cloned.1.call-update) | async-done | bytes 589840 | tf_op jit(solution)/shard_map/reduce_scatter | solution.py:260
  1012.0 173.6 %reduce-scatter.21.cloned.1.call-done = f32[768,192]{0,1:T(8,128)} async-done(((f32[768,3072]{0,1:T(8,128)}), f32[768,192]{0,1:T(8,128)}) %reduce-scatter.21.cloned.1.call-update) | async-done | bytes 589840 | tf_op jit(solution)/shard_map/reduce_scatter | solution.py:259
  1187.5 174.8 %reduce-scatter.19.cloned.1.call-done = f32[768,192]{0,1:T(8,128)} async-done(((f32[768,3072]{0,1:T(8,128)}), f32[768,192]{0,1:T(8,128)}) %reduce-scatter.19.cloned.1.call-update) | async-done | bytes 589840 | tf_op jit(solution)/shard_map/reduce_scatter | solution.py:258
  1364.2 8.2 fusion.50
  1372.3 39.3 %psum.87 = f32[32,12]{0,1:T(8,128)} all-reduce(f32[32,12]{0,1:T(8,128)} %fusion.50), channel_id=1, replica_groups=mesh['tower'=2,'batch'=16] {'tower','batch'}, use_global_device_ids=true, to_apply=%region_36.37 | all-reduce | flops 384 | bytes 3072 | tf_op jit(solution)/shard_map/psum | solution.py:277
  1411.7 2.7 fusion.52
  (212 shorter events, 82.1 us)
Async XLA Ops:
  7.2 11.1 copy-start
  7.2 273.2 %reduce-scatter.9.cloned.1.call-start = ((), (), s32[]{:S(2)}) async-start(), calls=%async_computation.8 | async-start | bytes 417792 | tf_op jit(solution)/shard_map/reduce_scatter | solution.py:190
  7.3 5.0 copy-start.45
  18.3 36.0 %copy-start.7 = (bf16[512,768]{0,1:T(8,128)(2,1)}, bf16[512,768]{0,1:T(8,128)(2,1)S(1)}, u32[]{:S(2)}) copy-start(bf16[512,768]{0,1:T(8,128)(2,1)S(1)} %copy.69) | copy-start | bytes 2359300
  21.4 41.5 %copy-start.9 = (bf16[512,768]{0,1:T(8,128)(2,1)}, bf16[512,768]{0,1:T(8,128)(2,1)S(1)}, u32[]{:S(2)}) copy-start(bf16[512,768]{0,1:T(8,128)(2,1)S(1)} %copy.67) | copy-start | bytes 2359300
  61.0 5.4 copy-start.1
  62.9 5.5 copy-start.25
  62.9 7.4 slice-start
  69.4 9.1 copy-start.15
  70.3 8.2 slice-start.4
  73.0 5.5 copy-start.14
  73.0 5.5 slice-start.5
  81.3 200.3 %copy-start.4 = (f32[512,768]{1,0:T(8,128)}, f32[512,768]{1,0:T(8,128)S(1)}, u32[]{:S(2)}) copy-start(f32[512,768]{1,0:T(8,128)S(1)} %get-tuple-element.115) | copy-start | bytes 4718596
  162.8 317.7 %reduce-scatter.17.cloned.1.call-start = ((), (), s32[]{:S(2)}) async-start(), calls=%async_computation.12 | async-start | bytes 2506752 | tf_op jit(solution)/shard_map/reduce_scatter | solution.py:257
  284.3 14.0 slice-start.2
  284.3 16.7 %slice-start.8 = ((s8[4718592]{0:T(1024)(128)(4,1)}), s8[524288]{0:T(1024)(128)(4,1)S(1)}, s32[]{:S(2)}) async-start(s8[4718592]{0:T(1024)(128)(4,1)} %bitcast.157), calls=%async_computation.25 | async-start | bytes 1048576
  287.8 10.5 slice-start.3
  287.8 13.2 slice-start.9
  308.0 260.2 %reduce-scatter.15.cloned.1.call-start = ((), (), s32[]{:S(2)}) async-start(), calls=%async_computation.11 | async-start | bytes 2506752 | tf_op jit(solution)/shard_map/reduce_scatter | solution.py:256
  324.1 377.2 %reduce-scatter.11.cloned.1.call-start = ((), (), s32[]{:S(2)}) async-start(), calls=%async_computation.9 | async-start | bytes 2506752 | tf_op jit(solution)/shard_map/reduce_scatter | solution.py:254
  324.1 8.1 copy-start.26
  332.2 7.0 copy-start.8
  345.1 488.7 %reduce-scatter.13.cloned.1.call-start = ((), (), s32[]{:S(2)}) async-start(), calls=%async_computation.10 | async-start | bytes 2506752 | tf_op jit(solution)/shard_map/reduce_scatter | solution.py:255
  353.5 656.8 %reduce-scatter.23.cloned.1.call-start = ((), (), s32[]{:S(2)}) async-start(), calls=%async_computation.15 | async-start | bytes 10027008 | tf_op jit(solution)/shard_map/reduce_scatter | solution.py:260
  360.6 825.1 %reduce-scatter.21.cloned.1.call-start = ((), (), s32[]{:S(2)}) async-start(), calls=%async_computation.14 | async-start | bytes 10027008 | tf_op jit(solution)/shard_map/reduce_scatter | solution.py:259
  369.9 992.4 %reduce-scatter.19.cloned.1.call-start = ((), (), s32[]{:S(2)}) async-start(), calls=%async_computation.13 | async-start | bytes 10027008 | tf_op jit(solution)/shard_map/reduce_scatter | solution.py:258
  378.2 1036.2 %all-reduce.8.cloned.1.call-start = ((), (), s32[]{:S(2)}) async-start(), calls=%async_computation.16 | async-start | bytes 2359296 | tf_op jit(solution)/shard_map/psum | solution.py:266
  380.9 14.4 %copy-start.13 = (bf16[12,64,512]{2,1,0:T(8,128)(2,1)S(1)}, bf16[12,64,512]{2,1,0:T(8,128)(2,1)}, u32[]{:S(2)}) copy-start(bf16[12,64,512]{2,1,0:T(8,128)(2,1)} %copy-done.12) | copy-start | bytes 2359300
  1364.1 47.5 %copy-start.6 = (f32[512,768]{1,0:T(8,128)S(1)}, f32[512,768]{1,0:T(8,128)}, u32[]{:S(2)}) copy-start(f32[512,768]{1,0:T(8,128)} %copy-done.5) | copy-start | bytes 4718596
  1364.1 47.5 %copy-start.42 = (f32[512]{0:T(512)S(1)}, f32[512]{0:T(512)}, u32[]{:S(2)}) copy-start(f32[512]{0:T(512)} %get-tuple-element.100) | copy-start | bytes 6148
  1414.4 8.1 copy-start.30
  1414.4 9.0 copy-start.29
  (41 other events, 87.2 us)
Sparse Core Ops, SparseCore 0:
  162.9 117.4 reduce-scatter.8
  308.1 127.6 reduce-scatter.16
  440.7 127.3 reduce-scatter.14
  573.6 127.6 reduce-scatter.10
  706.1 127.6 reduce-scatter.12
  840.3 169.9 reduce-scatter.22
  1015.9 169.7 reduce-scatter.20
  1192.3 169.9 reduce-scatter.18
  1366.3 19.0 all-reduce.7
where the time goes:
time: 1440 us; the launch traced here: 1430 us
  waiting for transfers between devices  989 us (69%)
  blocking collectives  194 us (13%)
  matrix products  136 us (9%)
  local copies, waits for them, and re-layouts  49.3 us (3%)
  other arithmetic  45.6 us (3%)
  between operations  15.8 us (1%)
    reduce_scatter x1, waiting for transfers between devices, body(): lax.psum_scatter(grad_w_down, 'batch', scatter_dimension=1, tiled=True)  175 us
    reduce_scatter x1, waiting for transfers between devices, body(): lax.psum_scatter(grad_w_gate, 'batch', scatter_dimension=1, tiled=True)  175 us
    reduce_scatter x1, waiting for transfers between devices, body(): lax.psum_scatter(grad_w_up, 'batch', scatter_dimension=1, tiled=True)  174 us
    reduce_scatter x1, waiting for transfers between devices, body(): lax.psum_scatter(grad_w_query, 'batch', scatter_dimension=1, tiled=True)  132 us
    reduce_scatter x1, waiting for transfers between devices, body(): lax.psum_scatter(grad_w_key, 'batch', scatter_dimension=1, tiled=True)  131 us
    reduce_scatter x1, waiting for transfers between devices, body(): lax.psum_scatter(doc_terms, 'batch', scatter_dimension=0, tiled=True)  117 us
    reduce_scatter x1, waiting for transfers between devices, body(): lax.psum_scatter(grad_w_value, 'batch', scatter_dimension=1, tiled=True)  86.1 us
    all_gather x1, blocking collectives, body(): gathered = lax.all_gather(unit_vec, ('tower', 'batch'), axis=0, tiled=True)  77 us
  transfers between devices with their start and end apart: 9, of which 7 were waited for; matrix products, arithmetic and copies ran while one was open for 8% of the time, Pallas kernels for 0%

commit v1 on v0

v1 whole, which is shorter than its diff:
```python
import functools

import jax
import jax.numpy as jnp
import numpy as np
from jax import lax
from jax.experimental import pallas as pl
from jax.experimental.pallas import tpu as pltpu
from jax.sharding import PartitionSpec as P

ITEMS = 8
eps_norm = 1e-06
temper = 0.05
max_distance = 128
highest = lax.Precision.HIGHEST
masked_value = -1000000000.0
contract_rows = (((0,), (0,)), ((), ()))
contract_cols = (((1,), (1,)), ((), ()))
f32 = jnp.float32
bf16 = jnp.bfloat16
LANES = 128
VMEM_BYTES = 56 * 1024 * 1024
TINY = pl.CostEstimate(flops=1024, bytes_accessed=1024, transcendentals=0)


def bucket_of(relative, bucket_count):
    halfway = bucket_count // 2
    upper_part = np.where(relative > 0, halfway, 0)
    distance = np.abs(relative)
    exact_span = halfway // 2
    scaled = (
        np.log(np.maximum(distance, 1) / exact_span)
        / np.log(max_distance / exact_span)
        * (halfway - exact_span)
    )
    far_bucket = np.minimum(
        exact_span + np.floor(np.maximum(scaled, 0.0)).astype(np.int32), halfway - 1
    )
    return (upper_part + np.where(distance < exact_span, distance, far_bucket)).astype(np.int32)


def one_hot(buckets, bucket_count):
    return (buckets[:, None] == np.arange(bucket_count)[None, :]).astype(np.float32)


def near_offsets():
    lane = np.arange(4 * LANES)
    return np.where(lane < 3 * LANES, lane - LANES, lane - 5 * LANES)


def rms_scale(values):
    return lax.rsqrt(jnp.mean(values * values, axis=-1, keepdims=True) + eps_norm)


def norm_back(values, scale, gain, grad_normed):
    scaled_grad = grad_normed * gain
    grad_values = scale * scaled_grad - values * scale**3 * jnp.mean(
        scaled_grad * values, axis=-1, keepdims=True
    )
    grad_gain = jnp.sum(grad_normed * values * scale, axis=0, keepdims=True)
    return (grad_values, grad_gain)


def project(left, right):
    return jnp.dot(left, right, preferred_element_type=f32)


def dot_f32(left, right, dims):
    return lax.dot_general(left, right, dims, preferred_element_type=f32)


def dot_exact(left, right):
    return jnp.dot(left, right, precision=highest, preferred_element_type=f32)


def params(**more):
    return pltpu.CompilerParams(vmem_limit_bytes=VMEM_BYTES, **more)


def shape_of(dims, kind):
    return jax.ShapeDtypeStruct(dims, kind)


def whole(array):
    zeros = (0,) * len(array.shape)
    return pl.BlockSpec(array.shape, lambda *_: zeros)


def half_lanes(block, side):
    lane = lax.broadcasted_iota(jnp.int32, block.shape, 1)
    keep = lane < LANES // 2 if side == 0 else lane >= LANES // 2
    return jnp.where(keep, block, jnp.zeros_like(block))


def attn_fwd_kernel(
    x_ref, gain_a_ref, gain_f_ref, wq_ref, wk_ref, wv_ref, wo_ref, seg_col_ref, seg_row_ref, base_ref,
    normed_ref, q_ref, k_ref, v_ref, probs_ref, mixed_ref, middle_ref, normed_ffn_ref,
):
    step = pl.program_id(0)
    length = x_ref.shape[0]
    blocks = length // LANES

    @pl.when(step == 0)
    def _():
        x = x_ref[...].astype(f32)
        normed_ref[...] = (x * rms_scale(x) * gain_a_ref[...]).astype(bf16)
        middle_ref[...] = x

    normed = normed_ref[...]
    query = project(normed, wq_ref[...]).astype(bf16)
    key = project(normed, wk_ref[...]).astype(bf16)
    value = project(normed, wv_ref[...]).astype(bf16)
    q_ref[...] = query
    k_ref[...] = key
    v_ref[...] = value
    near, far = [], []
    for side in range(2):
        base = base_ref[0, side : side + 1, :]
        spread = jnp.broadcast_to(base, (LANES, 4 * LANES))
        near.append(pltpu.roll(spread, 0, 1, stride=1, stride_axis=0))
        far.append((base[:, 3 * LANES + 1 : 3 * LANES + 2], base[:, 3 * LANES - 1 : 3 * LANES]))
    for ib in range(blocks):
        rows = slice(ib * LANES, (ib + 1) * LANES)
        same = seg_col_ref[rows, :] == seg_row_ref[...]
        out = []
        for side in range(2):
            logits = dot_f32(half_lanes(query[rows, :], side), key, contract_cols)
            tiles = []
            for jb in range(blocks):
                if jb - ib < -1:
                    tile = jnp.broadcast_to(far[side][0], (LANES, LANES))
                elif jb - ib > 1:
                    tile = jnp.broadcast_to(far[side][1], (LANES, LANES))
                else:
                    at = (jb - ib + 1) * LANES
                    tile = near[side][:, at : at + LANES]
                tiles.append(tile)
            logits = jnp.where(same, logits + jnp.concatenate(tiles, axis=1), masked_value)
            peak = jnp.max(logits, axis=1, keepdims=True)
            weight = jnp.exp(logits - peak)
            total = jnp.sum(weight, axis=1, keepdims=True)
            probs = (weight * (1.0 / total)).astype(bf16)
            probs_ref[side, rows, :] = probs
            out.append(project(probs, value))
        lane = lax.broadcasted_iota(jnp.int32, (LANES, LANES), 1)
        mixed_ref[rows, :] = jnp.where(lane < LANES // 2, out[0], out[1]).astype(bf16)
    middle_ref[...] += project(mixed_ref[...], wo_ref[...])

    @pl.when(step == pl.num_programs(0) - 1)
    def _():
        middle = middle_ref[...]
        normed_ffn_ref[...] = (middle * rms_scale(middle) * gain_f_ref[...]).astype(bf16)


def attn_fwd(x, gain_a, gain_f, w_query, w_key, w_value, w_output, seg_col, seg_row, base):
    length, width = x.shape
    pairs = width // LANES
    pair = pl.BlockSpec((length, LANES), lambda h: (0, h))
    column = pl.BlockSpec((width, LANES), lambda h: (0, h))
    low = shape_of((length, width), bf16)
    high = shape_of((length, width), f32)
    base = base.reshape(pairs, 2, 4 * LANES)
    return pl.pallas_call(
        attn_fwd_kernel,
        grid=(pairs,),
        in_specs=[
            whole(x),
            whole(gain_a),
            whole(gain_f),
            column,
            column,
            column,
            pl.BlockSpec((LANES, width), lambda h: (h, 0)),
            whole(seg_col),
            whole(seg_row),
            pl.BlockSpec((1, 2, 4 * LANES), lambda h: (h, 0, 0)),
        ],
        out_specs=[
            whole(low),
            pair,
            pair,
            pair,
            pl.BlockSpec((2, length, length), lambda h: (h, 0, 0)),
            pair,
            whole(high),
            whole(low),
        ],
        out_shape=[low, low, low, low, shape_of((2 * pairs, length, length), bf16), low, high, low],
        compiler_params=params(),
        cost_estimate=TINY,
        name="attn_fwd",
    )(x, gain_a, gain_f, w_query, w_key, w_value, w_output, seg_col, seg_row, base)


def attn_bwd_kernel(q_ref, k_ref, v_ref, g_ref, probs_ref, gq_ref, gk_ref, gv_ref, sums_ref, grad_scr):
    length = q_ref.shape[0]
    blocks = length // LANES
    key = k_ref[...]
    value = v_ref[...]
    gq, gk, gv, sums = [], [], [], []
    row = lax.broadcasted_iota(jnp.int32, (LANES, LANES), 0)
    column = lax.broadcasted_iota(jnp.int32, (LANES, LANES), 1)
    flip = (row + column == LANES - 1).astype(f32)
    for side in range(2):
        near = [None, None, None]
        far = [None, None]
        parts = []
        for ib in range(blocks):
            rows = slice(ib * LANES, (ib + 1) * LANES)
            grad_mixed = half_lanes(g_ref[rows, :], side)
            grad_probs = dot_f32(grad_mixed, value, contract_cols)
            probs = probs_ref[side, rows, :].astype(f32)
            inner = jnp.sum(probs * grad_probs, axis=1, keepdims=True)
            grad_low = (probs * (grad_probs - inner)).astype(bf16)
            grad_scr[rows, :] = grad_low
            parts.append(project(grad_low, key))
            wide = grad_low.astype(f32)
            for jb in range(blocks):
                tile = wide[:, jb * LANES : (jb + 1) * LANES]
                if abs(jb - ib) <= 1:
                    into, at = near, jb - ib + 1
                else:
                    into, at = far, 0 if jb < ib else 1
                into[at] = tile if into[at] is None else into[at] + tile
        gq.append(jnp.concatenate(parts, axis=0))
        half = slice(side * LANES // 2, (side + 1) * LANES // 2)
        gk.append(project(q_ref[...].T[half, :], grad_scr[...]))
        gv.append(project(g_ref[...].T[half, :], probs_ref[side]))
        spread = dot_exact(flip, jnp.concatenate(near, axis=1))
        spread = jnp.concatenate([spread, jnp.zeros_like(near[0])], axis=1)
        skew = pltpu.roll(spread, 0, 1, stride=1, stride_axis=0)
        sums.append(jnp.sum(skew, axis=0, keepdims=True))
        lows = [jnp.sum(tile, axis=0, keepdims=True) for tile in far]
        sums.append(jnp.concatenate(lows + [jnp.zeros((1, 2 * LANES), f32)], axis=1))
    lane = lax.broadcasted_iota(jnp.int32, (length, LANES), 1)
    gq_ref[...] = jnp.where(lane < LANES // 2, gq[0], gq[1]).astype(bf16)
    gk_ref[...] = jnp.concatenate(gk, axis=0).astype(bf16).T
    gv_ref[...] = jnp.concatenate(gv, axis=0).astype(bf16).T
    sums_ref[0] = jnp.concatenate(sums, axis=0)


def attn_bwd(query, key, value, grad_mixed, probs):
    length, width = query.shape
    pairs = width // LANES
    pair = pl.BlockSpec((length, LANES), lambda h: (0, h))
    low = shape_of((length, width), bf16)
    return pl.pallas_call(
        attn_bwd_kernel,
        grid=(pairs,),
        in_specs=[pair, pair, pair, pair, pl.BlockSpec((2, length, length), lambda h: (h, 0, 0))],
        out_specs=[pair, pair, pair, pl.BlockSpec((1, 4, 4 * LANES), lambda h: (h, 0, 0))],
        out_shape=[low, low, low, shape_of((pairs, 4, 4 * LANES), f32)],
        scratch_shapes=[pltpu.VMEM((length, length), bf16)],
        compiler_params=params(),
        cost_estimate=TINY,
        name="attn_bwd",
    )(query, key, value, grad_mixed, probs)


def attn_in_kernel(
    gq_ref, gk_ref, gv_ref, wq_ref, wk_ref, wv_ref, x_ref, middle_ref, gain_ref, sums_ref, near_ref, far_ref,
    gain_f_ref, gain_l_ref, tokens_ref, small_ref,
):
    grad_normed = dot_f32(gq_ref[...], wq_ref[...], contract_cols)
    grad_normed += dot_f32(gk_ref[...], wk_ref[...], contract_cols)
    grad_normed += dot_f32(gv_ref[...], wv_ref[...], contract_cols)
    x = x_ref[...].astype(f32)
    grad_in, grad_gain = norm_back(x, rms_scale(x), gain_ref[...], grad_normed)
    tokens_ref[...] = (middle_ref[...] + grad_in).astype(bf16)
    heads = sums_ref.shape[0]
    table = dot_exact(sums_ref[:, 0, :], near_ref[...]) + dot_exact(sums_ref[:, 1, :], far_ref[...])
    each = x_ref.shape[1] // LANES
    small_ref[...] = jnp.zeros_like(small_ref)
    for index, gain in enumerate((grad_gain, gain_f_ref[...], gain_l_ref[...])):
        for r in range(each):
            small_ref[index * each + r : index * each + r + 1, :] = gain[:, r * LANES : (r + 1) * LANES]
    small_ref[3 * each : 3 * each + heads, :] = table


def attn_in(gq, gk, gv, w_query, w_key, w_value, x, grad_middle, gain, sums, near_hot, far_hot, gain_f, gain_l):
    args = (gq, gk, gv, w_query, w_key, w_value, x, grad_middle, gain, sums, near_hot, far_hot, gain_f, gain_l)
    rows = 3 * (x.shape[1] // LANES) + sums.shape[0]
    outs = [shape_of(x.shape, bf16), shape_of((-(-rows // 8) * 8, LANES), f32)]
    return pl.pallas_call(
        attn_in_kernel,
        grid=(1,),
        in_specs=[whole(a) for a in args],
        out_specs=[whole(o) for o in outs],
        out_shape=outs,
        compiler_params=params(),
        cost_estimate=TINY,
        name="attn_in",
    )(*args)


def gelu_parts(gate):
    c = np.float32(np.sqrt(2.0 / np.pi))
    cube = np.float32(0.044715 * np.sqrt(2.0 / np.pi))
    square = gate * gate
    half = 0.5 * jnp.tanh(gate * (c + cube * square)) + 0.5
    act = gate * half
    slope = half + act * (1.0 - half) * (2 * c + 6 * cube * square)
    return act, slope


def ffn_fwd_kernel(
    normed_ref, middle_ref, wg_ref, wu_ref, wd_ref, seg_row_ref, gain_ref, score_ref,
    hidden_ref, act_ref, coef_ref, full_ref, out_ref, pooled_ref, pack_ref,
):
    step = pl.program_id(0)

    @pl.when(step == 0)
    def _():
        full_ref[...] = middle_ref[...]

    normed = normed_ref[...]
    gate = project(normed, wg_ref[...])
    up = project(normed, wu_ref[...])
    act, slope = gelu_parts(gate)
    hidden = (act * up).astype(bf16)
    hidden_ref[...] = hidden
    act_ref[...] = act.astype(bf16)
    coef_ref[...] = (up * slope).astype(bf16)
    full_ref[...] += project(hidden, wd_ref[...])

    @pl.when(step == pl.num_programs(0) - 1)
    def _():
        full = full_ref[...]
        out_ref[...] = full.astype(bf16)
        final_norm = full * rms_scale(full) * gain_ref[...]
        item = lax.broadcasted_iota(jnp.int32, (ITEMS, full.shape[0]), 0) + 1
        member = (item == seg_row_ref[...]).astype(f32)
        pooled = dot_exact(member, final_norm) / jnp.sum(member, axis=1, keepdims=True)
        pooled_ref[...] = pooled
        inv_length = lax.rsqrt(jnp.sum(pooled * pooled, axis=1, keepdims=True) + eps_norm)
        parts = [(pooled * inv_length).astype(bf16)]
        rest = score_ref[...]
        for _ in range(3):
            parts.append(rest.astype(bf16))
            rest = rest - parts[-1].astype(f32)
        pack = jnp.concatenate(parts, axis=1)
        for b in range(pack_ref.shape[0]):
            pack_ref[b] = pack


def ffn_fwd(normed, middle, w_gate, w_up, w_down, seg_row, gain, score_grad, n, block=512):
    length, width = normed.shape
    wide = w_gate.shape[1]
    weight = pl.BlockSpec((width, block), lambda j: (0, j))
    column = pl.BlockSpec((length, block), lambda j: (0, j))
    low = shape_of((length, wide), bf16)
    outs = [
        low,
        low,
        low,
        shape_of((length, width), f32),
        shape_of((length, width), bf16),
        shape_of((ITEMS, width), f32),
        shape_of((n, ITEMS, width + 3 * score_grad.shape[1]), bf16),
    ]
    return pl.pallas_call(
        ffn_fwd_kernel,
        grid=(wide // block,),
        in_specs=[
            whole(normed),
            whole(middle),
            weight,
            weight,
            pl.BlockSpec((block, width), lambda j: (j, 0)),
            whole(seg_row),
            whole(gain),
            whole(score_grad),
        ],
        out_specs=[column, column, column] + [whole(o) for o in outs[3:]],
        out_shape=outs,
        compiler_params=params(),
        cost_estimate=TINY,
        name="ffn_fwd",
    )(normed, middle, w_gate, w_up, w_down, seg_row, gain, score_grad)


def ffn_back_kernel(
    at_ref, own_ref, got_ref, full_ref, og_ref, pooled_ref, seg_col_ref, seg_row_ref, gain_ref, wd_ref, act_ref, coef_ref,
    scores_ref, ffn_grad_ref, grad_out_ref, gain_l_ref, keep_ref, send_ref, units_scr, turned_scr,
):
    step = pl.program_id(0)
    tower = at_ref[0]
    me = at_ref[1]
    length, width = full_ref.shape
    n = own_ref.shape[0]

    @pl.when(step == 0)
    def _():
        items = n * ITEMS
        for b in range(n):
            units_scr[b * ITEMS : (b + 1) * ITEMS, :] = got_ref[b, :, :width].astype(f32)
        theirs = units_scr[...].astype(bf16)
        for b in range(n):
            rows = slice(b * ITEMS, (b + 1) * ITEMS)
            units_scr[rows, :] = own_ref[b, :, :width].astype(f32)
            turned_scr[rows, :] = sum(
                own_ref[b, :, width + k * items : width + (k + 1) * items].astype(f32) for k in range(3)
            )
        ours = units_scr[...].astype(bf16)
        queries = jnp.where(tower == 0, ours, theirs)
        docs = jnp.where(tower == 0, theirs, ours)
        units_scr[...] = queries.astype(f32)
        mine = pl.ds(pl.multiple_of(me * ITEMS, ITEMS), ITEMS)
        scores_ref[...] = dot_f32(units_scr[mine, :].astype(bf16), docs, contract_cols) / temper
        score_grad = turned_scr[...]
        turned_scr[...] = jnp.where(tower == 0, score_grad, score_grad.T)
        grad_unit = dot_exact(turned_scr[mine, :], theirs.astype(f32)) / temper
        pooled = pooled_ref[...]
        inv_length = lax.rsqrt(jnp.sum(pooled * pooled, axis=1, keepdims=True) + eps_norm)
        grad_pooled = inv_length * grad_unit - pooled * inv_length**3 * jnp.sum(
            grad_unit * pooled, axis=1, keepdims=True
        )
        item = lax.broadcasted_iota(jnp.int32, (ITEMS, length), 0) + 1
        count = jnp.sum((item == seg_row_ref[...]).astype(f32), axis=1, keepdims=True)
        item = lax.broadcasted_iota(jnp.int32, (length, ITEMS), 1) + 1
        grad_final = dot_exact((item == seg_col_ref[...]).astype(f32), grad_pooled / count)
        full = full_ref[...]
        back, gain_l_ref[...] = norm_back(full, rms_scale(full), gain_ref[...], grad_final)
        grad_output = og_ref[...].astype(f32) + back
        grad_out_ref[...] = grad_output
        ffn_grad_ref[...] = grad_output.astype(bf16)

    grad_hidden = dot_f32(ffn_grad_ref[...], wd_ref[...], contract_cols)
    grad_gate = (grad_hidden * coef_ref[...].astype(f32)).astype(bf16)
    grad_up = (grad_hidden * act_ref[...].astype(f32)).astype(bf16)

    @pl.when(tower == 0)
    def _():
        keep_ref[...] = grad_gate
        send_ref[...] = grad_up

    @pl.when(tower != 0)
    def _():
        keep_ref[...] = grad_up
        send_ref[...] = grad_gate


def ffn_back(at, own, got, full, out_grad, pooled, seg_col, seg_row, gain, w_down, act, coef, block=512):
    length, width = full.shape
    wide = act.shape[1]
    n = own.shape[0]
    items = n * ITEMS
    column = pl.BlockSpec((length, block), lambda j, s: (0, j))
    low = shape_of((length, wide), bf16)
    outs = [
        shape_of((ITEMS, items), f32),
        shape_of((length, width), bf16),
        shape_of((length, width), f32),
        shape_of((1, width), f32),
        low,
        low,
    ]
    args = (own, got, full, out_grad, pooled, seg_col, seg_row, gain)
    return pl.pallas_call(
        ffn_back_kernel,
        grid_spec=pltpu.PrefetchScalarGridSpec(
            num_scalar_prefetch=1,
            grid=(wide // block,),
            in_specs=[whole(a) for a in args]
            + [pl.BlockSpec((block, width), lambda j, s: (j, 0)), column, column],
            out_specs=[whole(o) for o in outs[:4]] + [column, column],
            scratch_shapes=[pltpu.VMEM((items, width), f32), pltpu.VMEM((items, items), f32)],
        ),
        out_shape=outs,
        compiler_params=params(),
        cost_estimate=TINY,
        name="ffn_back",
    )(at, *args, w_down, act, coef)


def mid_back_kernel(
    at_ref, keep_ref, send_ref, wg_ref, wu_ref, middle_ref, gain_ref, grad_out_ref, wo_ref,
    grad_middle_ref, attn_grad_ref, grad_mixed_ref, gain_f_ref, total_scr,
):
    step = pl.program_id(0)
    first = at_ref[0] == 0
    keep = keep_ref[...]
    send = send_ref[...]
    term = dot_f32(jnp.where(first, keep, send), wg_ref[...], contract_cols)
    term += dot_f32(jnp.where(first, send, keep), wu_ref[...], contract_cols)

    @pl.when(step == 0)
    def _():
        total_scr[...] = term

    @pl.when(step != 0)
    def _():
        total_scr[...] += term

    @pl.when(step == pl.num_programs(0) - 1)
    def _():
        middle = middle_ref[...]
        back, gain_f_ref[...] = norm_back(middle, rms_scale(middle), gain_ref[...], total_scr[...])
        grad_middle = grad_out_ref[...] + back
        grad_middle_ref[...] = grad_middle
        attn_grad = grad_middle.astype(bf16)
        attn_grad_ref[...] = attn_grad
        grad_mixed_ref[...] = dot_f32(attn_grad, wo_ref[...], contract_cols).astype(bf16)


def mid_back(at, keep, send, w_gate, w_up, middle, gain, grad_output, w_output, block=512):
    length, width = middle.shape
    wide = keep.shape[1]
    column = pl.BlockSpec((length, block), lambda j, s: (0, j))
    weight = pl.BlockSpec((width, block), lambda j, s: (0, j))
    outs = [
        shape_of((length, width), f32),
        shape_of((length, width), bf16),
        shape_of((length, width), bf16),
        shape_of((1, width), f32),
    ]
    args = (middle, gain, grad_output, w_output)
    return pl.pallas_call(
        mid_back_kernel,
        grid_spec=pltpu.PrefetchScalarGridSpec(
            num_scalar_prefetch=1,
            grid=(wide // block,),
            in_specs=[column, column, weight, weight] + [whole(a) for a in args],
            out_specs=[whole(o) for o in outs],
            scratch_shapes=[pltpu.VMEM((length, width), f32)],
        ),
        out_shape=outs,
        compiler_params=params(),
        cost_estimate=TINY,
        name="mid_back",
    )(at, keep, send, w_gate, w_up, *args)


def reversed_bits(value, count):
    out = 0
    for k in range(count):
        out = out | (((value >> k) & 1) << (count - 1 - k))
    return out


def bit_order(first, bits):
    return [first, 1 - first] + list(range(2, bits))


def grad_pieces(mats, pieces, n, at):
    bits = n.bit_length() - 1
    widths = [lefts[0].shape[1] // n for lefts, _, _, _ in mats]
    inner = None
    if all(w % 16 == 0 for w in widths):
        for cand in (4, 8, 16, 32):
            if cand <= n and all(cand * w % LANES == 0 for w in widths):
                inner = cand
                break
    if inner is None:
        return grad_pieces_plain(mats, pieces, n, at)
    groups = n // inner
    inner_count = inner.bit_length() - 1
    flat, in_specs, counts, spans = [], [], [], []
    for (lefts, rights, halved, _), width in zip(mats, widths):
        for left in lefts:
            flat.append(left)
            in_specs.append(pl.BlockSpec((left.shape[0], inner * width), lambda g, m: (0, g)))
        for right in rights:
            flat.append(right)
            span = right.shape[1] // 2 if halved else right.shape[1]
            if halved:
                in_specs.append(pl.BlockSpec((right.shape[0], span), lambda g, m: (0, m[0])))
            else:
                in_specs.append(whole(right))
        counts.append(len(lefts))
        spans.append(span)

    def place(g, m):
        return (0, reversed_bits(g ^ (m[1] // inner), bits - inner_count), 0, 0)

    out_shape, out_specs = [], []
    for _, rows, lanes in pieces:
        for _ in range(2):
            out_shape.append(shape_of((inner // 2, groups, rows, lanes), bf16))
            out_specs.append(pl.BlockSpec((inner // 2, 1, rows, lanes), place))
    dests = [d for _, _, _, d in mats]
    scratch = [pltpu.VMEM((inner, w, span), bf16) for w, span in zip(widths, spans)]

    def kernel(at_ref, *refs):
        ins = refs[: len(flat)]
        outs = refs[len(flat) : len(flat) + len(out_shape)]
        scrs = refs[len(flat) + len(out_shape) :]
        own = at_ref[1] % inner
        at_in = 0
        for index, count in enumerate(counts):
            total = None
            for k in range(count):
                term = dot_f32(ins[at_in + k][...], ins[at_in + count + k][...], contract_rows)
                total = term if total is None else total + term
            at_in += 2 * count
            low = total.astype(bf16)
            width = widths[index]
            for i in range(inner):
                scrs[index][i] = low[i * width : (i + 1) * width]
            for piece, offset, lanes in dests[index]:
                first = pieces[piece][0]
                order = bit_order(first, inner_count)
                for slot in range(inner):
                    pos = sum(((slot >> (inner_count - 1 - k)) & 1) << bit for k, bit in enumerate(order))
                    out = outs[2 * piece + (0 if slot >= inner // 2 else 1)]
                    out[slot % (inner // 2), 0, offset : offset + width, :] = scrs[index][pos ^ own][:, lanes]

    res = pl.pallas_call(
        kernel,
        grid_spec=pltpu.PrefetchScalarGridSpec(
            num_scalar_prefetch=1,
            grid=(groups,),
            in_specs=in_specs,
            out_specs=out_specs,
            scratch_shapes=scratch,
        ),
        out_shape=out_shape,
        compiler_params=params(),
        cost_estimate=TINY,
        name="weight_grads",
    )(at, *flat)
    found = []
    for index, (first, rows, lanes) in enumerate(pieces):
        found.append((res[2 * index], res[2 * index + 1], bit_order(first, bits)[1:]))
    return found


def grad_pieces_plain(mats, pieces, n, at):
    bits = n.bit_length() - 1
    order = jnp.arange(n, dtype=jnp.int32) ^ at[1]
    filled = [[] for _ in pieces]
    for lefts, rights, halved, dests in mats:
        if halved:
            span = rights[0].shape[1] // 2
            rights = [lax.dynamic_slice_in_dim(r, at[0] * span, span, 1) for r in rights]
        total = sum(dot_f32(a, b, contract_rows) for a, b in zip(lefts, rights)).astype(bf16)
        total = jnp.take(total.reshape(n, -1, total.shape[1]), order, axis=0)
        for piece, offset, lanes in dests:
            filled[piece].append((offset, total[:, :, lanes]))
    found = []
    for (first, rows, lanes), parts in zip(pieces, filled):
        parts = [p for _, p in sorted(parts, key=lambda p: p[0])]
        joined = jnp.concatenate(parts, axis=1)
        tail = joined.shape[1:]
        sequence = bit_order(first, bits)
        joined = joined.reshape((2,) * bits + tail)
        joined = joined.transpose([bits - 1 - b for b in sequence] + [bits, bits + 1])
        found.append((joined[1], joined[0], sequence[1:]))
    return found


def swap(values, bit, n):
    return lax.ppermute(values, "batch", [(i, i ^ (1 << bit)) for i in range(n)])


def swap_tower(values):
    return lax.ppermute(values, "tower", [(0, 1), (1, 0)])


def after(values, *others):
    return lax.optimization_barrier((values,) + others)[0]


class Part:
    def __init__(self, held, bits):
        self.held = held
        self.bits = bits

    def total(self, which):
        return sum(h[which].astype(f32) for h in self.held)


def open_pieces(pieces, firsts, n):
    parts = []
    for (send, keep, bits), first in zip(pieces, firsts):
        shape = (2,) * len(bits) + send.shape[-2:]
        got = swap(send, first, n)
        parts.append(Part([keep.reshape(shape), got.reshape(shape)], bits))
    return parts


def to_send(parts):
    return [part.total(1).astype(bf16) for part in parts]


def exchange(parts, sends, n):
    return [
        Part([h[0] for h in part.held] + [swap(send, part.bits[0], n)], part.bits[1:])
        for part, send in zip(parts, sends)
    ]


def to_send_joined(parts, dim):
    return jnp.concatenate(to_send(parts), axis=dim)


def exchange_joined(parts, send, dim, n):
    got = swap(send, parts[0].bits[0], n)
    at, found = 0, []
    for part in parts:
        size = part.held[0].shape[dim]
        piece = lax.slice_in_dim(got, at, at + size, axis=got.ndim + dim)
        found.append(Part([h[0] for h in part.held] + [piece], part.bits[1:]))
        at += size
    return found


def hold(parts, *others):
    return [Part(part.held[:-1] + [after(part.held[-1], *others)], part.bits) for part in parts]


def finish(parts, dim):
    return jnp.concatenate([sum(h.astype(f32) for h in part.held) for part in parts], axis=dim).astype(bf16)


def body(
    n,
    tokens,
    segments,
    w_query,
    w_key,
    w_value,
    w_output,
    w_gate,
    w_up,
    w_down,
    gain_attn,
    gain_ffn,
    gain_final,
    bias_table,
    out_grad,
    score_grad,
):
    length = tokens.shape[2]
    width = tokens.shape[3]
    wide = w_gate.shape[1]
    heads = bias_table.shape[1]
    buckets = bias_table.shape[0]
    bits = n.bit_length() - 1
    half = width // 2
    quarter = wide // 4
    narrow = width // n
    tower = lax.axis_index("tower")
    at = jnp.stack([tower, lax.axis_index("batch")]).astype(jnp.int32)
    x = tokens.reshape(length, width)
    seg_col = segments.reshape(length, 1)
    seg_row = segments.reshape(1, length)
    gain_attn = gain_attn.reshape(1, width)
    gain_ffn = gain_ffn.reshape(1, width)
    gain_final = gain_final.reshape(1, width)

    near_hot = jnp.asarray(one_hot(bucket_of(near_offsets(), buckets), buckets))
    base = lax.dot_general(bias_table, near_hot, (((0,), (1,)), ((), ())), precision=highest)
    normed, query, key, value, probs, mixed, middle, normed_ffn = attn_fwd(
        x, gain_attn, gain_ffn, w_query, w_key, w_value, w_output, seg_col, seg_row, base
    )
    hidden, act, coef, full, output, pooled, pack = ffn_fwd(
        normed_ffn, middle, w_gate, w_up, w_down, seg_row, gain_final, score_grad, n
    )
    packs = lax.all_to_all(pack, "batch", 0, 0, tiled=True)
    normed_got = swap_tower(normed)
    mixed_got = swap_tower(mixed)
    ffn_got = swap_tower(normed_ffn)
    hidden_got = swap_tower(hidden)
    packs_got = swap_tower(packs)
    packs_got = after(packs_got, normed_got, mixed_got, ffn_got, hidden_got)

    scores, ffn_grad, grad_output, grad_gain_final, pair_own, pair_send = ffn_back(
        at, packs, packs_got, full, out_grad.reshape(length, width), pooled, seg_col, seg_row, gain_final, w_down, act, coef
    )
    ffn_grad_got = swap_tower(ffn_grad)
    pair_got = swap_tower(pair_send)

    down = grad_pieces(
        [
            (
                [ffn_grad, ffn_grad_got],
                [hidden, hidden_got],
                True,
                [(0, 0, slice(0, quarter)), (1, 0, slice(quarter, 2 * quarter))],
            )
        ],
        [(0, narrow, quarter), (1, narrow, quarter)],
        n,
        at,
    )
    down_parts = open_pieces(down, (0, 1), n)
    pair_got = after(pair_got, down[0][0], down[1][0])
    wide_grads = grad_pieces(
        [
            (
                [pair_own, pair_got],
                [normed_ffn, ffn_got],
                False,
                [(0, 0, slice(0, half)), (1, 0, slice(half, width))],
            )
        ],
        [(0, wide // n, half), (1, wide // n, half)],
        n,
        at,
    )

    down_parts = hold(down_parts, wide_grads[0][0])
    sends = to_send(down_parts)
    wide_parts = open_pieces([(after(w[0], *sends),) + w[1:] for w in wide_grads], (0, 1), n)
    down_parts = exchange(down_parts, sends, n)
    grad_middle, attn_grad, grad_mixed, grad_gain_ffn = mid_back(
        at, after(pair_own, *sends), pair_send, w_gate, w_up, middle, gain_ffn, grad_output, w_output
    )
    attn_grad_got = swap_tower(attn_grad)
    grad_query, grad_key, grad_value, sums = attn_bwd(query, key, value, grad_mixed, probs)
    grad_query_got = swap_tower(grad_query)
    grad_key_got = swap_tower(grad_key)
    grad_value_got = swap_tower(grad_value)
    wide_parts = hold(wide_parts, grad_query)
    sends = to_send(wide_parts)
    wide_parts = exchange(wide_parts, sends, n)
    down_parts = hold(down_parts, *sends)
    send = to_send_joined(down_parts, -1)
    down_parts = exchange_joined(down_parts, send, -1, n)
    attn = grad_pieces(
        [
            ([grad_query, grad_query_got], [normed, normed_got], True, [(0, 0, slice(0, half))]),
            ([grad_key, grad_key_got], [normed, normed_got], True, [(0, narrow, slice(0, half))]),
            ([grad_value, after(grad_value_got, send)], [normed, normed_got], True, [(1, 0, slice(0, half))]),
            ([attn_grad, attn_grad_got], [mixed, mixed_got], True, [(1, narrow, slice(0, half))]),
        ],
        [(0, 2 * narrow, half), (1, 2 * narrow, half)],
        n,
        at,
    )
    attn_parts = open_pieces(attn, (0, 1), n)
    wide_parts = hold(wide_parts, attn[0][0])
    send = to_send_joined(wide_parts, -1)
    wide_parts = exchange_joined(wide_parts, send, -1, n)
    down_parts = hold(down_parts, send)
    send = to_send_joined(down_parts, -1)
    down_parts = exchange_joined(down_parts, send, -1, n)

    near_sums = jnp.asarray(
        np.pad(one_hot(bucket_of(np.arange(4 * LANES) - (2 * LANES - 1), buckets), buckets), ((0, 0), (0, LANES - buckets)))
    )
    far_sums = np.zeros((4 * LANES, LANES), np.float32)
    far_sums[:LANES, buckets // 2 - 1] = 1.0
    far_sums[LANES : 2 * LANES, buckets - 1] = 1.0
    grad_tokens, small = attn_in(
        after(grad_query, send), grad_key, grad_value, w_query, w_key, w_value, x, grad_middle, gain_attn,
        sums.reshape(heads, 2, 4 * LANES), near_sums, jnp.asarray(far_sums), grad_gain_ffn, grad_gain_final,
    )
    attn_parts = hold(attn_parts, grad_tokens)
    sends = to_send(attn_parts)
    attn_parts = exchange(attn_parts, sends, n)
    small = after(small, *sends) + swap_tower(small)
    small = jnp.broadcast_to(small[None], (n,) + small.shape)
    wide_parts = hold(wide_parts, small)
    last = small
    while wide_parts[0].bits:
        send = to_send_joined(wide_parts, -1)
        wide_parts = exchange_joined(wide_parts, send, -1, n)
        if down_parts[0].bits:
            down_parts = hold(down_parts, send)
            send = to_send_joined(down_parts, -1)
            down_parts = exchange_joined(down_parts, send, -1, n)
        attn_parts = hold(attn_parts, send)
        send = to_send_joined(attn_parts, -2)
        attn_parts = exchange_joined(attn_parts, send, -2, n)
        last = send
        if wide_parts[0].bits:
            wide_parts = hold(wide_parts, last)
    small = lax.all_to_all(after(small, last), "batch", 0, 0, tiled=True)
    down_own = finish(hold(down_parts, last), -1)
    wide_own = finish(hold(wide_parts, down_own), -1)
    small = jnp.sum(after(small, wide_own), axis=0)
    each = width // LANES
    gains = small[: 3 * each].reshape(3, width)
    gains = lax.dynamic_slice_in_dim(gains, at[1] * narrow, narrow, 1)
    grad_bias_table = small[3 * each : 3 * each + heads, :buckets].T
    attn_parts = hold(attn_parts, small)
    while attn_parts[0].bits:
        attn_parts = exchange_joined(attn_parts, to_send_joined(attn_parts, -2), -2, n)

    def both(own):
        got = swap_tower(own)
        first = jnp.where(tower == 0, own, got).astype(f32)
        second = jnp.where(tower == 0, got, own).astype(f32)
        return first, second

    grad_w_down = jnp.concatenate(both(down_own), axis=1).T
    gate_t, up_t = both(wide_own)
    attn_t = jnp.concatenate(both(finish(attn_parts, -2)), axis=1)
    return (
        output.reshape(tokens.shape),
        scores,
        grad_tokens.reshape(tokens.shape),
        attn_t[:narrow].T,
        attn_t[narrow : 2 * narrow].T,
        attn_t[2 * narrow : 3 * narrow].T,
        attn_t[3 * narrow :].T,
        gate_t.T,
        up_t.T,
        grad_w_down,
        gains[0],
        gains[1],
        gains[2],
        grad_bias_table,
    )


def solution(mesh):
    row = P("tower", "batch", None, None)
    in_specs = (row, P("tower", "batch", None)) + (P(),) * 11 + (row, P("batch", None))
    out_specs = (row, P("batch", None), row) + (P(None, "batch"),) * 7 + (P("batch"),) * 3 + (P(),)
    return jax.shard_map(
        functools.partial(body, mesh.shape["batch"]),
        mesh=mesh,
        in_specs=in_specs,
        out_specs=out_specs,
        check_vma=False,
    )
```

time: 1440 us -> 255 us (0.18)
  waiting for transfers between devices: 989 us -> 50.3 us
  blocking collectives: 194 us -> 0 us
  matrix products: 136 us -> 1.29 us
  Pallas kernels: 0 us -> 130 us
  local copies, waits for them, and re-layouts: 49.3 us -> 16.8 us
  starting transfers between devices: 1.01 us -> 31.7 us
  other arithmetic: 45.6 us -> 22.7 us
  between operations: 15.8 us -> 1.27 us
    reduce_scatter x8 -> x0, waiting for transfers between devices: 989 us -> none  [the longest x1 175 us: body(): lax.psum_scatter(grad_w_down, 'batch', scatter_dimension=1, tiled=True)]
    dot_general x34 -> x1, matrix products: 136 us -> 1.29 us  [body(): lax.dot_general(bias_table, near_hot, (((0,), (1,)), ((), ())), precision...]
    pallas_call x0 -> x9, Pallas kernels: none -> 130 us  [the longest x1 28.4 us: attn_fwd(): pl.pallas_call(attn_fwd_kernel, grid=(pairs,), in_specs=[whole(x), whole(...]
    all_gather x1 -> x0, blocking collectives: 77 us -> none  [body(): gathered = lax.all_gather(unit_vec, ('tower', 'batch'), axis=0, tiled=True)]
    unnamed x1 -> x0, blocking collectives: 75 us -> none
    psum x2 -> x0, blocking collectives: 42.1 us -> none  [the longest x1 39.3 us: body(): grad_bias_table = lax.psum(grad_bias_local, ('tower', 'batch'))]
    ppermute x0 -> x33, waiting for transfers between devices: none -> 39.8 us  [the longest x18 32 us: swap(): return lax.ppermute(values, 'batch', [(i, i ^ 1 << bit) for i in range(n)])]
    convert_element_type x5 -> x0, local copies, waits for them, and re-layouts: 19.6 us -> none  [the longest x1 14.4 us: attend_back(): grad_logits = (attn_probs * (grad_probs - inner_sum)).astype(jnp.bfloat16)]
  transfers between devices with their start and end apart: 9 -> 35, of which waited for: 7 -> 10; matrix products, arithmetic and copies ran while one was open for 8% -> 10% of each run, Pallas kernels for 0% -> 27%
where the time goes in v1:
time: 255 us; the launch traced here: 254 us
  Pallas kernels  130 us (51%)
  waiting for transfers between devices  50.3 us (20%)
  starting transfers between devices  31.7 us (12%)
  other arithmetic  22.7 us (9%)
  local copies, waits for them, and re-layouts  16.8 us (7%)
    ppermute x18, waiting for transfers between devices, swap(): return lax.ppermute(values, 'batch', [(i, i ^ 1 << bit) for i in range(n)])  32 us
    pallas_call x1, Pallas kernels, attn_fwd(): pl.pallas_call(attn_fwd_kernel, grid=(pairs,), in_specs=[whole(x), whole(...  28.4 us
    pallas_call x3, Pallas kernels, grad_pieces(): pl.pallas_call(kernel, grid_spec=pltpu.PrefetchScalarGridSpec(num_scalar_...  26.3 us
    pallas_call x1, Pallas kernels, attn_bwd(): pl.pallas_call(attn_bwd_kernel, grid=(pairs,), in_specs=[pair, pair, pair...  20.7 us
    pallas_call x1, Pallas kernels, ffn_fwd(): pl.pallas_call(ffn_fwd_kernel, grid=(wide // block,), in_specs=[whole(nor...  17.1 us
    ppermute x18, starting transfers between devices, swap(): return lax.ppermute(values, 'batch', [(i, i ^ 1 << bit) for i in range(n)])  16.4 us
    pallas_call x1, Pallas kernels, mid_back(): pl.pallas_call(mid_back_kernel, grid_spec=pltpu.PrefetchScalarGridSpec(nu...  15.3 us
    pallas_call x1, Pallas kernels, ffn_back(): pl.pallas_call(ffn_back_kernel, grid_spec=pltpu.PrefetchScalarGridSpec(nu...  14.7 us
  transfers between devices with their start and end apart: 35, of which 10 were waited for; matrix products, arithmetic and copies ran while one was open for 10% of the time, Pallas kernels for 27%

profile of v1, /device:TPU:0, one launch (start us, length us, event | category | flops | bytes accessed | tf_op | source)
XLA Modules:
  0.0 253.7 jit_solution(1107509384796917175)
XLA Ops:
  0.7 1.3 reshape.374.gain_a_ref.gain_ref
  1.9 1.3 reshape.375.gain_f_ref.gain_ref
  3.2 1.3 reshape.379.gain_ref
  4.5 1.3 convolution_bitcast_fusion
  6.4 1.5 copy.32.seg_col_ref
  7.9 28.4 %attn_fwd.1 = (bf16[512,768]{1,0:T(8,128)(2,1)}, bf16[512,768]{1,0:T(8,128)(2,1)}, bf16[512,768]{1,0:T(8,128)(2,1)}, bf16[512,768]{1,0:T(8,128)(2,1)}, bf16[12,5...) custom-call(bf16[512,768]{1,0:T(8,128)(2,1)} %bitcast.260, ...), custom_call_target="tpu_custom_call" | custom-call | flops 1024 | bytes 1024 | tf_op jit(solution)/shard_map/attn_fwd/pallas_call | solution.py:163
  36.4 17.1 %ffn_fwd.1 = (bf16[512,3072]{1,0:T(8,128)(2,1)}, bf16[512,3072]{1,0:T(8,128)(2,1)}, bf16[512,3072]{1,0:T(8,128)(2,1)}, f32[512,768]{1,0:T(8,128)}, bf16[512,768]...) custom-call(bf16[512,768]{1,0:T(8,128)(2,1)} %get-tuple-element.89.normed_ref.refs_2_, ...), custom_call_target="tpu_custom_call" | custom-call | flops 1024 | bytes 1024 | tf_op jit(solution)/shard_map/ffn_fwd/pallas_call | solution.py:361
  54.0 7.9 %all-to-all-start = ((bf16[16,8,1152]{2,1,0:T(8,128)(2,1)}), bf16[16,8,1152]{2,1,0:T(8,128)(2,1)S(1)}, u32[]{:S(2)}, u32[]{:S(2)}) async-start(bf16[16,8,1152]{2,1,0:T(8,128)(2,1)} %get-tuple-element.92), calls=%async_computation | async-start | bytes 589824 | tf_op jit(solution)/shard_map/all_to_all | solution.py:760
  62.7 10.5 %all-to-all-done.own_ref = bf16[16,8,1152]{2,1,0:T(8,128)(2,1)S(1)} async-done(((bf16[16,8,1152]{2,1,0:T(8,128)(2,1)}), bf16[16,8,1152]{2,1,0:T(8,128)(2,1)S(1)}, u32[]{:S(2)}, u32[]{:S(2)}) %all-to-all-start) | async-done | bytes 294944 | tf_op jit(solution)/shard_map/all_to_all | solution.py:760
  74.9 14.7 %ffn_back.1 = (f32[8,128]{1,0:T(8,128)}, bf16[512,768]{1,0:T(8,128)(2,1)}, f32[512,768]{1,0:T(8,128)}, f32[1,768]{1,0:T(1,128)}, bf16[512,3072]{1,0:T(8,128)(2,1)}, /*index=5*/bf16[512,3072]{1,0:T(8,128)(2,1)}) custom-call(s32[2]{0:T(128)} %pad_add_fusion.at_ref, bf16[16,8,1152]{2,1,0:T(8,128)(2,1)} %copy-done.13, ...), custom_call_target="tpu_custom_call" | custom-call | flops 1024 | bytes 1024 | tf_op jit(solution)/shard_map/ffn_back/pallas_call | solution.py:459
  90.2 6.5 %collective-permute-done.5.refs_1_ = bf16[512,768]{1,0:T(8,128)(2,1)S(1)} collective-permute-done((bf16[512,768]{1,0:T(8,128)(2,1)}, bf16[512,768]{1,0:T(8,128)(2,1)S(1)}, u32[]{:S(2)}, u32[]{:S(2)}) %collective-permute-start.5) | collective-permute-done | bytes 786464 | tf_op jit(solution)/shard_map/ppermute | solution.py:657
  97.7 7.0 %weight_grads.3 = (bf16[4,2,48,768]{3,2,1,0:T(8,128)(2,1)}, bf16[4,2,48,768]{3,2,1,0:T(8,128)(2,1)}, bf16[4,2,48,768]{3,2,1,0:T(8,128)(2,1)}, bf16[4,2,48,768]{3,2,1,0:T(8,128)(2,1)}) custom-call(s32[2]{0:T(128)} %pad_add_fusion.at_ref, bf16[512,768]{1,0:T(8,128)(2,1)} %get-tuple-element.106.refs_0_, bf16[512,768]{1,0:T(8,128)(2,1)} %copy-done.17, ...), custom_call_target="tpu_custom_call" | custom-call | flops 1024 | bytes 1024 | tf_op jit(solution)/shard_map/weight_grads/pallas_call | solution.py:608
  106.0 1.6 copy-done.4
  107.6 10.3 %weight_grads.4 = (bf16[2,4,192,384]{3,2,1,0:T(8,128)(2,1)}, bf16[2,4,192,384]{3,2,1,0:T(8,128)(2,1)}, bf16[2,4,192,384]{3,2,1,0:T(8,128)(2,1)}, bf16[2,4,192,384]{3,2,1,0:T(8,128)(2,1)}) custom-call(s32[2]{0:T(128)} %pad_add_fusion.at_ref, bf16[512,3072]{1,0:T(8,128)(2,1)} %get-tuple-element.116.refs_0_.keep_ref, bf16[512,3072]{1,0:T(8,128)(2,1)} %copy-done.4, ...), custom_call_target="tpu_custom_call" | custom-call | flops 1024 | bytes 1024 | tf_op jit(solution)/shard_map/weight_grads/pallas_call | solution.py:608
  117.9 2.4 collective-permute-done.8
  121.6 1.3 collective-permute-start.11
  122.8 1.5 collective-permute-start.12
  125.1 15.3 %mid_back.1 = (f32[512,768]{1,0:T(8,128)}, bf16[512,768]{1,0:T(8,128)(2,1)}, bf16[512,768]{1,0:T(8,128)(2,1)}, f32[1,768]{1,0:T(1,128)}) custom-call(s32[2]{0:T(128)} %pad_add_fusion.at_ref, bf16[512,3072]{1,0:T(8,128)(2,1)} %get-tuple-element.116.refs_0_.keep_ref, bf16[512,3072]{1,0:T(8,128)(2,1)} %get-tuple-element.109.send_ref, bf16[768,3072]{1,0:T(8,128)(2,1)} %wg_ref.3, ...), custom_call_target="tpu_custom_call" | custom-call | flops 1024 | bytes 1024 | tf_op jit(solution)/shard_map/mid_back/pallas_call | solution.py:518
  140.4 20.7 %attn_bwd.1 = (bf16[512,768]{1,0:T(8,128)(2,1)}, bf16[512,768]{1,0:T(8,128)(2,1)}, bf16[512,768]{1,0:T(8,128)(2,1)}, f32[6,4,512]{2,1,0:T(4,128)}) custom-call(bf16[512,768]{1,0:T(8,128)(2,1)} %get-tuple-element.102.q_ref, bf16[512,768]{1,0:T(8,128)(2,1)} %get-tuple-element.103.k_ref, bf16[512,768]{1,0:T(8,128)(2,1)} %get-tuple-element.104.v_ref, ...), custom_call_target="tpu_custom_call" | custom-call | flops 1024 | bytes 1024 | tf_op jit(solution)/shard_map/attn_bwd/pallas_call | solution.py:247
  166.4 1.3 collective-permute-start.14
  171.5 9.1 %weight_grads.5 = (bf16[4,2,96,384]{3,2,1,0:T(8,128)(2,1)}, bf16[4,2,96,384]{3,2,1,0:T(8,128)(2,1)}, bf16[4,2,96,384]{3,2,1,0:T(8,128)(2,1)}, bf16[4,2,96,384]{3,2,1,0:T(8,128)(2,1)}) custom-call(s32[2]{0:T(128)} %pad_add_fusion.at_ref, bf16[512,768]{1,0:T(8,128)(2,1)} %get-tuple-element.139.refs_0_.gq_ref, ...), custom_call_target="tpu_custom_call" | custom-call | flops 1024 | bytes 1024 | tf_op jit(solution)/shard_map/weight_grads/pallas_call | solution.py:608
  181.4 1.2 collective-permute-start.20
  183.6 1.2 fusion.5
  184.8 1.7 collective-permute-done.19
  191.7 7.1 %attn_in.1 = (bf16[512,768]{1,0:T(8,128)(2,1)}, f32[32,128]{1,0:T(8,128)}) custom-call(bf16[512,768]{1,0:T(8,128)(2,1)} %get-tuple-element.139.refs_0_.gq_ref, bf16[512,768]{1,0:T(8,128)(2,1)} %get-tuple-element.130.refs_4_.gk_ref, bf16[512,768]{1,0:T(8,128)(2,1)} %get-tuple-element.131.refs_8_.gv_ref, bf16[768,768]{1,0:T(8,128)(2,1)} %wq_ref.3, ...), custom_call_target="tpu_custom_call" | custom-call | flops 1024 | bytes 1024 | tf_op jit(solution)/shard_map/attn_in/pallas_call | solution.py:284
  199.4 1.2 collective-permute-start.21
  200.7 6.1 %collective-permute-done.22 = bf16[2,192,768]{2,1,0:T(8,128)(2,1)S(1)} collective-permute-done((bf16[2,192,768]{2,1,0:T(8,128)(2,1)S(1)}, bf16[2,192,768]{2,1,0:T(8,128)(2,1)S(1)}, u32[]{:S(2)}, u32[]{:S(2)}) %collective-permute-start.22) | collective-permute-done | bytes 589856 | tf_op jit(solution)/shard_map/ppermute | solution.py:653
  211.3 1.2 fusion.25
  213.0 2.1 collective-permute-start.27
  215.1 4.3 %all-to-all-start.1 = ((f32[16,32,128]{2,1,0:T(8,128)}), f32[16,32,128]{2,1,0:T(8,128)S(1)}, u32[]{:S(2)}, u32[]{:S(2)}) async-start(f32[16,32,128]{2,1,0:T(8,128)} %broadcast_in_dim.2), calls=%async_computation.1 | async-start | bytes 524288 | tf_op jit(solution)/shard_map/all_to_all | solution.py:870
  221.2 12.0 %collective-permute-done.27 = bf16[192,768]{1,0:T(8,128)(2,1)} collective-permute-done((bf16[192,768]{1,0:T(8,128)(2,1)}, bf16[192,768]{1,0:T(8,128)(2,1)}, u32[]{:S(2)}, u32[]{:S(2)}) %collective-permute-start.27) | collective-permute-done | bytes 294944 | tf_op jit(solution)/shard_map/ppermute | solution.py:653
  241.0 9.2 %collective-permute-done.29 = bf16[192,384]{1,0:T(8,128)(2,1)S(1)} collective-permute-done((bf16[192,384]{1,0:T(8,128)(2,1)S(1)}, bf16[192,384]{1,0:T(8,128)(2,1)S(1)}, u32[]{:S(2)}, u32[]{:S(2)}) %collective-permute-start.29) | collective-permute-done | bytes 147488 | tf_op jit(solution)/shard_map/ppermute | solution.py:653
  (171 shorter events, 43.0 us)
Async XLA Ops:
  53.5 21.5 %collective-permute-start.4 = (bf16[512,3072]{1,0:T(8,128)(2,1)}, bf16[512,3072]{1,0:T(8,128)(2,1)}, u32[]{:S(2)}, u32[]{:S(2)}) collective-permute-start(bf16[512,3072]{1,0:T(8,128)(2,1)} %get-tuple-element.95.refs_2_), channel_id=1, source_target_pairs={{0,16},{16,0},{1,17},{17,1},{2,18},{18,2},{3,19},{19,3},{4,20},{20... | collective-permute-start | bytes 9437192 | tf_op jit(solution)/shard_map/ppermute | solution.py:657
  54.0 19.2 %all-to-all-start = ((bf16[16,8,1152]{2,1,0:T(8,128)(2,1)}), bf16[16,8,1152]{2,1,0:T(8,128)(2,1)S(1)}, u32[]{:S(2)}, u32[]{:S(2)}) async-start(bf16[16,8,1152]{2,1,0:T(8,128)(2,1)} %get-tuple-element.92), calls=%async_computation | async-start | bytes 589824 | tf_op jit(solution)/shard_map/all_to_all | solution.py:760
  61.9 11.9 %collective-permute-start.1 = (bf16[512,768]{1,0:T(8,128)(2,1)S(1)}, bf16[512,768]{1,0:T(8,128)(2,1)S(1)}, u32[]{:S(2)}, u32[]{:S(2)}) collective-permute-start(bf16[512,768]{1,0:T(8,128)(2,1)S(1)} %copy-done.2), channel_id=1, source_target_pairs={{0,16},{16,0},{1,17},{17,1},{2,18},{18,2},{3,19},{19,3},{4,20},{20... | collective-permute-start | bytes 2359304 | tf_op jit(solution)/shard_map/ppermute | solution.py:657
  62.2 11.7 %collective-permute-start.2 = (bf16[512,768]{1,0:T(8,128)(2,1)S(1)}, bf16[512,768]{1,0:T(8,128)(2,1)}, u32[]{:S(2)}, u32[]{:S(2)}) collective-permute-start(bf16[512,768]{1,0:T(8,128)(2,1)S(1)} %copy-done.14), channel_id=1, source_target_pairs={{0,16},{16,0},{1,17},{17,1},{2,18},{18,2},{3,19},{19,3},{4,20},{20... | collective-permute-start | bytes 2359304 | tf_op jit(solution)/shard_map/ppermute | solution.py:657
  62.5 11.4 %collective-permute-start.3 = (bf16[512,768]{1,0:T(8,128)(2,1)S(1)}, bf16[512,768]{1,0:T(8,128)(2,1)}, u32[]{:S(2)}, u32[]{:S(2)}) collective-permute-start(bf16[512,768]{1,0:T(8,128)(2,1)S(1)} %copy-done.8), channel_id=1, source_target_pairs={{0,16},{16,0},{1,17},{17,1},{2,18},{18,2},{3,19},{19,3},{4,20},{20... | collective-permute-start | bytes 2359304 | tf_op jit(solution)/shard_map/ppermute | solution.py:657
  89.7 16.3 %collective-permute-start.7 = (bf16[512,3072]{1,0:T(8,128)(2,1)}, bf16[512,3072]{1,0:T(8,128)(2,1)S(1)}, u32[]{:S(2)}, u32[]{:S(2)}) collective-permute-start(bf16[512,3072]{1,0:T(8,128)(2,1)} %get-tuple-element.109.send_ref), channel_id=1, source_target_pairs={{0,16},{16,0},{1,17},{17,1},{2,18},{18,2},{3,19},{19,3},{4,20},{20... | collective-permute-start | bytes 9437192 | tf_op jit(solution)/shard_map/ppermute | solution.py:657
  89.9 6.8 %collective-permute-start.5 = (bf16[512,768]{1,0:T(8,128)(2,1)}, bf16[512,768]{1,0:T(8,128)(2,1)S(1)}, u32[]{:S(2)}, u32[]{:S(2)}) collective-permute-start(bf16[512,768]{1,0:T(8,128)(2,1)} %get-tuple-element.106.refs_0_), channel_id=1, source_target_pairs={{0,16},{16,0},{1,17},{17,1},{2,18},{18,2},{3,19},{19,3},{4,20},{20... | collective-permute-start | bytes 2359304 | tf_op jit(solution)/shard_map/ppermute | solution.py:657
  104.7 15.6 %collective-permute-start.8 = (bf16[4,2,48,768]{3,2,1,0:T(8,128)(2,1)}, bf16[4,2,48,768]{3,2,1,0:T(8,128)(2,1)S(1)}, u32[]{:S(2)}, u32[]{:S(2)}) collective-permute-start(bf16[4,2,48,768]{3,2,1,0:T(8,128)(2,1)} %get-tuple-element.110), channel_id=1, source_target_pairs={{0,2},{1,3},{2,0},{3,1},{4,6},{5,7},{6,4},{7,5},{8,10},{9,11},{10,... | collective-permute-start | bytes 1769480 | tf_op jit(solution)/shard_map/ppermute | solution.py:653
  105.5 15.3 %collective-permute-start.6 = (bf16[4,2,48,768]{3,2,1,0:T(8,128)(2,1)}, bf16[4,2,48,768]{3,2,1,0:T(8,128)(2,1)S(1)}, u32[]{:S(2)}, u32[]{:S(2)}) collective-permute-start(bf16[4,2,48,768]{3,2,1,0:T(8,128)(2,1)} %get-tuple-element.108), channel_id=1, source_target_pairs={{0,1},{1,0},{2,3},{3,2},{4,5},{5,4},{6,7},{7,6},{8,9},{9,8},{10,11... | collective-permute-start | bytes 1769480 | tf_op jit(solution)/shard_map/ppermute | solution.py:653
  121.0 41.3 %collective-permute-start.10 = (bf16[2,4,192,384]{3,2,1,0:T(8,128)(2,1)}, bf16[2,4,192,384]{3,2,1,0:T(8,128)(2,1)S(1)}, u32[]{:S(2)}, u32[]{:S(2)}) collective-permute-start(bf16[2,4,192,384]{3,2,1,0:T(8,128)(2,1)} %get-tuple-element.122), channel_id=1, source_target_pairs={{0,1},{1,0},{2,3},{3,2},{4,5},{5,4},{6,7},{7,6},{8,9},{9,8},{10,11... | collective-permute-start | bytes 3538952 | tf_op jit(solution)/shard_map/ppermute | solution.py:653
  121.6 42.2 %collective-permute-start.11 = (bf16[2,4,192,384]{3,2,1,0:T(8,128)(2,1)}, bf16[2,4,192,384]{3,2,1,0:T(8,128)(2,1)S(1)}, u32[]{:S(2)}, u32[]{:S(2)}) collective-permute-start(bf16[2,4,192,384]{3,2,1,0:T(8,128)(2,1)} %get-tuple-element.126), channel_id=1, source_target_pairs={{0,2},{1,3},{2,0},{3,1},{4,6},{5,7},{6,4},{7,5},{8,10},{9,11},{10,... | collective-permute-start | bytes 3538952 | tf_op jit(solution)/shard_map/ppermute | solution.py:653
  122.8 43.6 %collective-permute-start.12 = (bf16[2,2,48,768]{3,2,1,0:T(8,128)(2,1)S(1)}, bf16[2,2,48,768]{3,2,1,0:T(8,128)(2,1)}, u32[]{:S(2)}, u32[]{:S(2)}) collective-permute-start(bf16[2,2,48,768]{3,2,1,0:T(8,128)(2,1)S(1)} %fusion.6), channel_id=1, source_target_pairs={{0,1},{1,0},{2,3},{3,2},{4,5},{5,4},{6,7},{7,6},{8,9},{9,8},{10,11... | collective-permute-start | bytes 884744 | tf_op jit(solution)/shard_map/ppermute | solution.py:653
  124.3 40.7 %collective-permute-start.9 = (bf16[2,2,48,768]{3,2,1,0:T(8,128)(2,1)S(1)}, bf16[2,2,48,768]{3,2,1,0:T(8,128)(2,1)}, u32[]{:S(2)}, u32[]{:S(2)}) collective-permute-start(bf16[2,2,48,768]{3,2,1,0:T(8,128)(2,1)S(1)} %fusion.7), channel_id=1, source_target_pairs={{0,2},{1,3},{2,0},{3,1},{4,6},{5,7},{6,4},{7,5},{8,10},{9,11},{10,... | collective-permute-start | bytes 884744 | tf_op jit(solution)/shard_map/ppermute | solution.py:653
  162.2 6.7 %collective-permute-start.16 = (bf16[512,768]{1,0:T(8,128)(2,1)S(1)}, bf16[512,768]{1,0:T(8,128)(2,1)S(1)}, u32[]{:S(2)}, u32[]{:S(2)}) collective-permute-start(bf16[512,768]{1,0:T(8,128)(2,1)S(1)} %copy-done.6), channel_id=1, source_target_pairs={{0,16},{16,0},{1,17},{17,1},{2,18},{18,2},{3,19},{19,3},{4,20},{20... | collective-permute-start | bytes 2359304 | tf_op jit(solution)/shard_map/ppermute | solution.py:657
  162.5 9.0 %collective-permute-start.15 = (bf16[512,768]{1,0:T(8,128)(2,1)S(1)}, bf16[512,768]{1,0:T(8,128)(2,1)}, u32[]{:S(2)}, u32[]{:S(2)}) collective-permute-start(bf16[512,768]{1,0:T(8,128)(2,1)S(1)} %copy-done.5), channel_id=1, source_target_pairs={{0,16},{16,0},{1,17},{17,1},{2,18},{18,2},{3,19},{19,3},{4,20},{20... | collective-permute-start | bytes 2359304 | tf_op jit(solution)/shard_map/ppermute | solution.py:657
  163.8 6.2 %collective-permute-start.17 = (bf16[512,768]{1,0:T(8,128)(2,1)S(1)}, bf16[512,768]{1,0:T(8,128)(2,1)S(1)}, u32[]{:S(2)}, u32[]{:S(2)}) collective-permute-start(bf16[512,768]{1,0:T(8,128)(2,1)S(1)} %copy-done.7), channel_id=1, source_target_pairs={{0,16},{16,0},{1,17},{17,1},{2,18},{18,2},{3,19},{19,3},{4,20},{20... | collective-permute-start | bytes 2359304 | tf_op jit(solution)/shard_map/ppermute | solution.py:657
  165.0 6.5 %collective-permute-start.18 = (bf16[512,768]{1,0:T(8,128)(2,1)}, bf16[512,768]{1,0:T(8,128)(2,1)}, u32[]{:S(2)}, u32[]{:S(2)}) collective-permute-start(bf16[512,768]{1,0:T(8,128)(2,1)} %get-tuple-element.133.refs_12_), channel_id=1, source_target_pairs={{0,16},{16,0},{1,17},{17,1},{2,18},{18,2},{3,19},{19,3},{4,20},{20... | collective-permute-start | bytes 2359304 | tf_op jit(solution)/shard_map/ppermute | solution.py:657
  166.4 17.2 %collective-permute-start.14 = (bf16[2,2,192,384]{3,2,1,0:T(8,128)(2,1)}, bf16[2,2,192,384]{3,2,1,0:T(8,128)(2,1)}, u32[]{:S(2)}, u32[]{:S(2)}) collective-permute-start(bf16[2,2,192,384]{3,2,1,0:T(8,128)(2,1)} %fusion.1), channel_id=1, source_target_pairs={{0,2},{1,3},{2,0},{3,1},{4,6},{5,7},{6,4},{7,5},{8,10},{9,11},{10,... | collective-permute-start | bytes 1769480 | tf_op jit(solution)/shard_map/ppermute | solution.py:653
  168.9 13.7 %collective-permute-start.13 = (bf16[2,48,1536]{2,1,0:T(8,128)(2,1)S(1)}, bf16[2,48,1536]{2,1,0:T(8,128)(2,1)}, u32[]{:S(2)}, u32[]{:S(2)}) collective-permute-start(bf16[2,48,1536]{2,1,0:T(8,128)(2,1)S(1)} %pad_maximum_fusion.1), channel_id=1, source_target_pairs={{0,4},{1,5},{2,6},{3,7},{4,0},{5,1},{6,2},{7,3},{8,12},{9,13},{10,... | collective-permute-start | bytes 884744 | tf_op jit(solution)/shard_map/ppermute | solution.py:653
  169.9 16.6 %collective-permute-start.19 = (bf16[2,2,192,384]{3,2,1,0:T(8,128)(2,1)}, bf16[2,2,192,384]{3,2,1,0:T(8,128)(2,1)}, u32[]{:S(2)}, u32[]{:S(2)}) collective-permute-start(bf16[2,2,192,384]{3,2,1,0:T(8,128)(2,1)} %fusion), channel_id=1, source_target_pairs={{0,1},{1,0},{2,3},{3,2},{4,5},{5,4},{6,7},{7,6},{8,9},{9,8},{10,11... | collective-permute-start | bytes 1769480 | tf_op jit(solution)/shard_map/ppermute | solution.py:653
  180.6 18.2 %collective-permute-start.23 = (bf16[4,2,96,384]{3,2,1,0:T(8,128)(2,1)}, bf16[4,2,96,384]{3,2,1,0:T(8,128)(2,1)S(1)}, u32[]{:S(2)}, u32[]{:S(2)}) collective-permute-start(bf16[4,2,96,384]{3,2,1,0:T(8,128)(2,1)} %get-tuple-element.149), channel_id=1, source_target_pairs={{0,2},{1,3},{2,0},{3,1},{4,6},{5,7},{6,4},{7,5},{8,10},{9,11},{10,... | collective-permute-start | bytes 1769480 | tf_op jit(solution)/shard_map/ppermute | solution.py:653
  181.4 17.5 %collective-permute-start.20 = (bf16[4,2,96,384]{3,2,1,0:T(8,128)(2,1)}, bf16[4,2,96,384]{3,2,1,0:T(8,128)(2,1)S(1)}, u32[]{:S(2)}, u32[]{:S(2)}) collective-permute-start(bf16[4,2,96,384]{3,2,1,0:T(8,128)(2,1)} %get-tuple-element.134), channel_id=1, source_target_pairs={{0,1},{1,0},{2,3},{3,2},{4,5},{5,4},{6,7},{7,6},{8,9},{9,8},{10,11... | collective-permute-start | bytes 1769480 | tf_op jit(solution)/shard_map/ppermute | solution.py:653
  189.8 10.9 %collective-permute-start.28 = (bf16[48,1536]{1,0:T(8,128)(2,1)S(1)}, bf16[48,1536]{1,0:T(8,128)(2,1)S(1)}, u32[]{:S(2)}, u32[]{:S(2)}) collective-permute-start(bf16[48,1536]{1,0:T(8,128)(2,1)S(1)} %pad_maximum_fusion.5), channel_id=1, source_target_pairs={{0,8},{1,9},{2,10},{3,11},{4,12},{5,13},{6,14},{7,15},{8,0},{9,1},... | collective-permute-start | bytes 442376 | tf_op jit(solution)/shard_map/ppermute | solution.py:653
  190.7 16.1 %collective-permute-start.22 = (bf16[2,192,768]{2,1,0:T(8,128)(2,1)S(1)}, bf16[2,192,768]{2,1,0:T(8,128)(2,1)S(1)}, u32[]{:S(2)}, u32[]{:S(2)}) collective-permute-start(bf16[2,192,768]{2,1,0:T(8,128)(2,1)S(1)} %pad_maximum_fusion), channel_id=1, source_target_pairs={{0,4},{1,5},{2,6},{3,7},{4,0},{5,1},{6,2},{7,3},{8,12},{9,13},{10,... | collective-permute-start | bytes 1769480 | tf_op jit(solution)/shard_map/ppermute | solution.py:653
  199.0 11.4 %collective-permute-start.25 = (bf16[2,2,96,384]{3,2,1,0:T(8,128)(2,1)S(1)}, bf16[2,2,96,384]{3,2,1,0:T(8,128)(2,1)S(1)}, u32[]{:S(2)}, u32[]{:S(2)}) collective-permute-start(bf16[2,2,96,384]{3,2,1,0:T(8,128)(2,1)S(1)} %fusion.2), channel_id=1, source_target_pairs={{0,1},{1,0},{2,3},{3,2},{4,5},{5,4},{6,7},{7,6},{8,9},{9,8},{10,11... | collective-permute-start | bytes 884744 | tf_op jit(solution)/shard_map/ppermute | solution.py:653
  199.4 11.0 %collective-permute-start.21 = (bf16[2,2,96,384]{3,2,1,0:T(8,128)(2,1)S(1)}, bf16[2,2,96,384]{3,2,1,0:T(8,128)(2,1)S(1)}, u32[]{:S(2)}, u32[]{:S(2)}) collective-permute-start(bf16[2,2,96,384]{3,2,1,0:T(8,128)(2,1)S(1)} %fusion.3), channel_id=1, source_target_pairs={{0,2},{1,3},{2,0},{3,1},{4,6},{5,7},{6,4},{7,5},{8,10},{9,11},{10,... | collective-permute-start | bytes 884744 | tf_op jit(solution)/shard_map/ppermute | solution.py:653
  212.5 6.8 %collective-permute-start.32 = (bf16[48,1536]{1,0:T(8,128)(2,1)S(1)}, bf16[48,1536]{1,0:T(8,128)(2,1)}, u32[]{:S(2)}, u32[]{:S(2)}) collective-permute-start(bf16[48,1536]{1,0:T(8,128)(2,1)S(1)} %pad_maximum_fusion.6), channel_id=1, source_target_pairs={{0,16},{16,0},{1,17},{17,1},{2,18},{18,2},{3,19},{19,3},{4,20},{20... | collective-permute-start | bytes 442376 | tf_op jit(solution)/shard_map/ppermute | solution.py:657
  212.6 24.0 %collective-permute-start.26 = (bf16[2,192,384]{2,1,0:T(8,128)(2,1)}, bf16[2,192,384]{2,1,0:T(8,128)(2,1)}, u32[]{:S(2)}, u32[]{:S(2)}) collective-permute-start(bf16[2,192,384]{2,1,0:T(8,128)(2,1)} %pad_maximum_fusion.3), channel_id=1, source_target_pairs={{0,4},{1,5},{2,6},{3,7},{4,0},{5,1},{6,2},{7,3},{8,12},{9,13},{10,... | collective-permute-start | bytes 884744 | tf_op jit(solution)/shard_map/ppermute | solution.py:653
  213.0 20.2 %collective-permute-start.27 = (bf16[192,768]{1,0:T(8,128)(2,1)}, bf16[192,768]{1,0:T(8,128)(2,1)}, u32[]{:S(2)}, u32[]{:S(2)}) collective-permute-start(bf16[192,768]{1,0:T(8,128)(2,1)} %pad_maximum_fusion.2), channel_id=1, source_target_pairs={{0,8},{1,9},{2,10},{3,11},{4,12},{5,13},{6,14},{7,15},{8,0},{9,1},... | collective-permute-start | bytes 884744 | tf_op jit(solution)/shard_map/ppermute | solution.py:653
  215.1 22.6 %all-to-all-start.1 = ((f32[16,32,128]{2,1,0:T(8,128)}), f32[16,32,128]{2,1,0:T(8,128)S(1)}, u32[]{:S(2)}, u32[]{:S(2)}) async-start(f32[16,32,128]{2,1,0:T(8,128)} %broadcast_in_dim.2), calls=%async_computation.1 | async-start | bytes 524288 | tf_op jit(solution)/shard_map/all_to_all | solution.py:870
  236.6 14.9 %collective-permute-start.31 = (bf16[192,768]{1,0:T(8,128)(2,1)S(1)}, bf16[192,768]{1,0:T(8,128)(2,1)S(1)}, u32[]{:S(2)}, u32[]{:S(2)}) collective-permute-start(bf16[192,768]{1,0:T(8,128)(2,1)S(1)} %pad_maximum_fusion.4), channel_id=1, source_target_pairs={{0,16},{16,0},{1,17},{17,1},{2,18},{18,2},{3,19},{19,3},{4,20},{20... | collective-permute-start | bytes 884744 | tf_op jit(solution)/shard_map/ppermute | solution.py:657
  240.3 9.9 %collective-permute-start.29 = (bf16[192,384]{1,0:T(8,128)(2,1)S(1)}, bf16[192,384]{1,0:T(8,128)(2,1)S(1)}, u32[]{:S(2)}, u32[]{:S(2)}) collective-permute-start(bf16[192,384]{1,0:T(8,128)(2,1)S(1)} %pad_maximum_fusion.7), channel_id=1, source_target_pairs={{0,8},{1,9},{2,10},{3,11},{4,12},{5,13},{6,14},{7,15},{8,0},{9,1},... | collective-permute-start | bytes 442376 | tf_op jit(solution)/shard_map/ppermute | solution.py:653
  (35 other events, 293.6 us)
